TPU v7x, 256 devices: a whole 4x4x8 slice. The times are simulated.
256 devices in a mesh: out: 16 (over y, x_hi, core), inp: 16 (over x_lo, z).
Axes of the slice: x: 4 (x_hi: 2, x_lo: 2; x = x_hi * 2 + x_lo), y: 4, z: 8, core: 2. Of those that a mesh axis runs over, the one named last changes fastest.
Arguments:
- acts: bfloat16 [4096, 28672], P('out', 'inp'), may hold values from -6 to 6
- grads: bfloat16 [4096, 8192], P('out', 'inp'), may hold values from -6 to 6
- basis_in: bfloat16 [28672, 28672], P('inp', 'out'), may hold values from -0.03125 to 0.03125
- basis_out: bfloat16 [8192, 8192], P('inp', 'out'), may hold values from -0.0625 to 0.0625
- query_in: bfloat16 [28672, 512], P('out', 'inp'), may hold values from -0.03125 to 0.03125
- query_out: bfloat16 [8192, 512], P('out', 'inp'), may hold values from -0.0625 to 0.0625
- lengths: int32 [16], replicated, may hold values from 1 to 512, 4096 in all
Outputs:
- scores: float32 [16, 16], P(None, 'inp')
Inputs may be any that keep to these rules, and one draw needn't show every extreme that they name: Each example has at least one token, the lengths sum to 4096, and the longest has exactly 512 tokens.
All inputs are finite; a program needn't handle non-finite values.
Results may differ from a plain program's by a relative error of at most 0.0003.
Values may be sent and summed in bfloat16 or wider, within the bound.
No kernel may reach another device: no remote copies, remote signals or barrier semaphores. Data moves between devices by JAX's collectives and lax.ppermute only.
A program may use at most 64 MiB of HBM per device.

v0:
```python
import jax
import jax.numpy as jnp
from jax import lax
from jax.sharding import PartitionSpec as P

RANK = 32


def example_terms(per_token, position, lengths):
    finish = jnp.cumsum(lengths)
    starts = finish - lengths
    member = (
        (position[None, :] >= starts[:, None]) & (position[None, :] < finish[:, None])
    ).astype(jnp.float32)
    return jnp.dot(member, per_token, precision=lax.Precision.HIGHEST)


def per_device(acts, grads, basis_in, basis_out, query_in, query_out, lengths):
    pieces = lax.all_gather((query_in, query_out), "inp", axis=1, tiled=True)
    partial_in = jnp.dot(basis_in, pieces[0], preferred_element_type=jnp.float32)
    partial_out = jnp.dot(basis_out, pieces[1], preferred_element_type=jnp.float32)
    rotated_in, rotated_out = lax.psum((partial_in, partial_out), "out")
    input_side = jnp.dot(acts.astype(jnp.float32), rotated_in, precision=lax.Precision.HIGHEST)
    output_side = jnp.dot(grads.astype(jnp.float32), rotated_out, precision=lax.Precision.HIGHEST)
    token_count = acts.shape[0]
    first_token = lax.axis_index("out") * token_count
    side_in, side_out = (
        lax.psum_scatter(input_side, "inp", scatter_dimension=1, tiled=True),
        lax.psum_scatter(output_side, "inp", scatter_dimension=1, tiled=True),
    )
    local_queries = side_in.shape[1] // RANK
    per_token = jnp.sum((side_in * side_out).reshape(token_count, local_queries, RANK), axis=2)
    position = first_token + jnp.arange(token_count, dtype=jnp.int32)
    partial_value = example_terms(per_token, position, lengths)
    summed = lax.psum(partial_value, "out")
    return summed / lengths.astype(jnp.float32)[:, None]


def solution(mesh):
    placed = (
        P("out", "inp"),
        P("out", "inp"),
        P("inp", "out"),
        P("inp", "out"),
        P("out", "inp"),
        P("out", "inp"),
        P(),
    )
    return jax.shard_map(
        per_device, mesh=mesh, in_specs=placed, out_specs=P(None, "inp"), check_vma=False
    )
```

profile of v0, /device:TPU:1, one launch (start us, length us, event | category | flops | bytes accessed | tf_op | source)
XLA Modules:
  0.0 440.8 jit_solution(16456954884749358116)
XLA Ops:
  6.5 0.0 copy-start
  6.5 0.7 all-gather.2.cloned.1.call-update
  7.3 0.0 all-reduce.3.cloned.1.call-start
  7.3 35.3 %all_gather.7 = bf16[512,512]{0,1:T(8,128)(2,1)S(1)} all-gather(bf16[512,32]{0,1:T(8,128)(2,1)} %param.12), channel_id=1, replica_groups=mesh['out'=16,'inp'=16] {'inp'}, dimensions={1}, use_global_device_ids=true | all-gather | bytes 557056 | tf_op jit(solution)/shard_map/all_gather | solution.py:19
  42.6 2.6 fusion.5
  45.1 29.8 %all-gather.2.cloned.1.call-done = bf16[1792,512]{0,1:T(8,128)(2,1)} async-done(((bf16[1792,32]{0,1:T(8,128)(2,1)}), bf16[1792,512]{0,1:T(8,128)(2,1)}) %all-gather.2.cloned.1.call-update) | async-done | bytes 1835024 | tf_op jit(solution)/shard_map/all_gather | solution.py:19
  75.0 8.7 %fusion.4 = f32[1792,512]{1,0:T(8,128)} fusion(bf16[1792,1792]{1,0:T(8,128)(2,1)} %param.9, bf16[1792,512]{0,1:T(8,128)(2,1)} %all-gather.2.cloned.1.call-done), kind=kOutput, calls=%fused_computation.11 | convolution fusion | flops 3288334336 | bytes 11927552 | tf_op jit(solution)/shard_map/dot_general | solution.py:20
  83.7 0.0 all-reduce.3.cloned.1.call-update
  83.7 0.0 copy-start.2
  83.7 0.0 reduce-scatter.3.cloned.1.call-start
  83.8 168.9 %all-reduce.3.cloned.1.call-done = (f32[1792,512]{1,0:T(8,128)}, f32[512,512]{1,0:T(8,128)}) async-done(((f32[1792,512]{1,0:T(8,128)}, f32[512,512]{1,0:T(8,128)}), (f32[1792,512]{1,0:T(8,128)}, f32[512,512]{1,0:T(8,128)})) %all-reduce.3.cloned.1.call-update) | async-done | bytes 4718608 | tf_op jit(solution)/shard_map/psum | solution.py:22
  252.7 6.0 %convolution_bitcast_fusion.1 = f32[256,512]{0,1:T(8,128)} fusion(f32[1792,512]{1,0:T(8,128)} %get-tuple-element.5, bf16[256,1792]{1,0:T(8,128)(2,1)S(1)} %copy-done), kind=kOutput, calls=%fused_computation.1 | convolution fusion | flops 2818572288 | bytes 5111808 | tf_op jit(solution)/shard_map/dot_general | solution.py:23
  258.7 0.0 reduce-scatter.3.cloned.1.call-update
  258.7 0.0 reduce-scatter.5.cloned.1.call-start
  258.8 1.8 convolution_bitcast_fusion
  260.6 0.0 reduce-scatter.5.cloned.1.call-update
  260.6 0.1 copy.10
  260.8 0.1 reduce.2
  260.9 58.7 %reduce-scatter.3.cloned.1.call-done = f32[256,32]{0,1:T(8,128)} async-done(((f32[256,512]{0,1:T(8,128)}), f32[256,32]{0,1:T(8,128)}) %reduce-scatter.3.cloned.1.call-update) | async-done | bytes 32784 | tf_op jit(solution)/shard_map/reduce_scatter | solution.py:28
  319.6 68.9 %reduce-scatter.5.cloned.1.call-done = f32[256,32]{0,1:T(8,128)} async-done(((f32[256,512]{0,1:T(8,128)}), f32[256,32]{0,1:T(8,128)}) %reduce-scatter.5.cloned.1.call-update) | async-done | bytes 32784 | tf_op jit(solution)/shard_map/reduce_scatter | solution.py:29
  388.5 0.8 multiply_reduce_fusion
  389.3 0.2 convolution_bitcast_fusion.2
  389.5 44.3 %psum.23 = f32[16,1]{0,1:T(1,128)S(1)} all-reduce(f32[16,1]{0,1:T(1,128)S(1)} %convolution_bitcast_fusion.2), channel_id=1, replica_groups=mesh['out'=16,'inp'=16] {'out'}, use_global_device_ids=true, to_apply=%region_6.7 | all-reduce | flops 16 | bytes 128 | tf_op jit(solution)/shard_map/psum | solution.py:35
  433.7 0.5 bitcast_divide_fusion
  (10 shorter events, 0.1 us)
Async XLA Ops:
  6.5 246.2 %copy-start = (bf16[256,1792]{1,0:T(8,128)(2,1)S(1)}, bf16[256,1792]{1,0:T(8,128)(2,1)}, u32[]{:S(2)}) copy-start(bf16[256,1792]{1,0:T(8,128)(2,1)} %param.7) | copy-start | bytes 2752516
  6.5 68.5 %all-gather.2.cloned.1.call-start = ((), (), s32[]{:S(2)}) async-start(), calls=%async_computation.2 | async-start | bytes 1949696 | tf_op jit(solution)/shard_map/all_gather | solution.py:19
  7.3 245.5 %all-reduce.3.cloned.1.call-start = ((), (), s32[]{:S(2)}) async-start(), calls=%async_computation.5 | async-start | bytes 9437184 | tf_op jit(solution)/shard_map/psum | solution.py:22
  83.7 175.1 %copy-start.2 = (bf16[256,512]{1,0:T(8,128)(2,1)S(1)}, bf16[256,512]{1,0:T(8,128)(2,1)}, u32[]{:S(2)}) copy-start(bf16[256,512]{1,0:T(8,128)(2,1)} %param.8) | copy-start | bytes 786436
  83.7 235.8 %reduce-scatter.3.cloned.1.call-start = ((), (), s32[]{:S(2)}) async-start(), calls=%async_computation.3 | async-start | bytes 557056 | tf_op jit(solution)/shard_map/reduce_scatter | solution.py:28
  252.7 6.1 %copy-start.1 = (f32[512,512]{1,0:T(8,128)S(1)}, f32[512,512]{1,0:T(8,128)}, u32[]{:S(2)}) copy-start(f32[512,512]{1,0:T(8,128)} %get-tuple-element.6) | copy-start | bytes 3145732
  252.7 7.9 %copy-start.3 = (s32[16]{0:T(128)S(1)}, s32[16]{0:T(128)}, u32[]{:S(2)}) copy-start(s32[16]{0:T(128)} %param.13) | copy-start | bytes 196
  258.7 129.7 %reduce-scatter.5.cloned.1.call-start = ((), (), s32[]{:S(2)}) async-start(), calls=%async_computation.4 | async-start | bytes 557056 | tf_op jit(solution)/shard_map/reduce_scatter | solution.py:29
Sparse Core Ops, SparseCore 0:
  9.1 65.7 all-gather.1
  83.8 168.8 all-reduce.2
  258.9 60.6 reduce-scatter.2
  322.1 66.3 reduce-scatter.4
where the time goes:
time: 441 us
  waiting for transfers between devices  327 us (74%)
  blocking collectives  79.5 us (18%)
  matrix products  19.2 us (4%)
  between operations  13.2 us (3%)
    psum x1, waiting for transfers between devices, per_device(): rotated_in, rotated_out = lax.psum((partial_in, partial_out), 'out')  169 us
    reduce_scatter x1, waiting for transfers between devices, per_device(): lax.psum_scatter(output_side, 'inp', scatter_dimension=1, tiled=True)  68.9 us
    reduce_scatter x1, waiting for transfers between devices, per_device(): lax.psum_scatter(input_side, 'inp', scatter_dimension=1, tiled=True)  58.7 us
    psum x1, blocking collectives, per_device(): summed = lax.psum(partial_value, 'out')  44.3 us
    all_gather x1, blocking collectives, per_device(): pieces = lax.all_gather((query_in, query_out), 'inp', axis=1, tiled=True)  35.3 us
    all_gather x1, waiting for transfers between devices, per_device(): pieces = lax.all_gather((query_in, query_out), 'inp', axis=1, tiled=True)  29.8 us
  transfers between devices with their start and end apart: 4, of which 4 were waited for; matrix products, arithmetic and copies ran while one was open for 1% of the time, Pallas kernels for 0%

commit v1 on v0

v1 whole, which is shorter than its diff:
```python
import functools

import jax
import jax.numpy as jnp
from jax import lax
from jax.experimental import pallas as pl
from jax.experimental.pallas import tpu as pltpu
from jax.sharding import PartitionSpec as P

RANK = 32
LEVELS = 32700.0
STEPS = 64.0
PAD = 128
VMEM = pl.BlockSpec(memory_space=pltpu.VMEM)
SMEM = pl.BlockSpec(memory_space=pltpu.SMEM)


def params(mib):
    return pltpu.CompilerParams(vmem_limit_bytes=mib << 20)


def core_id():
    return lax.rem(lax.axis_index("out"), 2)


def level_of(x):
    largest = jnp.max(jnp.abs(x), axis=1, keepdims=True)
    return jnp.ceil(jnp.log2(jnp.maximum(largest, 1e-30)) * STEPS)


def encode(x, level):
    scaled = x * (jnp.exp2(level * (-1.0 / STEPS)) * LEVELS)
    scaled = jnp.clip(scaled, -32767.0, 32767.0)
    return jnp.round(scaled).astype(jnp.int32).astype(jnp.int16)


def unit_of(level):
    return jnp.exp2(level * (1.0 / STEPS)) * (1.0 / LEVELS)


def pack_levels(level_in, level_out):
    rows = level_in.shape[0]
    lane = lax.broadcasted_iota(jnp.int32, (rows, PAD), 1)
    both = jnp.where(lane < PAD // 2, level_in, level_out)
    return both.astype(jnp.int32).astype(jnp.int16)


def as_float(x):
    return x.astype(jnp.int32).astype(jnp.float32)


def units(tail):
    tail = as_float(tail)
    return unit_of(tail[:, 0:1]), unit_of(tail[:, PAD // 2 : PAD // 2 + 1])


def rotate_kernel(in_tiles, a_ref, b_ref, basis_in, basis_out, keep, send):
    step = pl.program_id(0)
    first = core_id() == 0
    width = basis_in.shape[1]
    contract = (((1,), (1,)), ((), ()))

    def run(lo, hi, basis):
        a, b = a_ref[:, lo:hi], b_ref[:, lo:hi]
        rows = jnp.concatenate([jnp.where(first, a, b), jnp.where(first, b, a)], axis=0)
        got = lax.dot_general(rows, basis[...], contract, preferred_element_type=jnp.float32)
        half = a.shape[0]
        keep[...] = got[:half]
        send[...] = got[half:]

    @pl.when(step < in_tiles)
    def _():
        run(0, width, basis_in)

    @pl.when(step >= in_tiles)
    def _():
        run(width, width + basis_out.shape[1], basis_out)


def rotate(a, b, basis_in, basis_out):
    tile = 256
    rows, width = a.shape
    in_tiles, out_tiles = basis_in.shape[0] // tile, basis_out.shape[0] // tile
    whole = pl.BlockSpec((rows, width), lambda i: (0, 0))
    result = pl.BlockSpec((rows, tile), lambda i: (0, i))
    shape = jax.ShapeDtypeStruct((rows, width), jnp.float32)
    flops = 4 * rows * (basis_in.size + basis_out.size)
    return pl.pallas_call(
        functools.partial(rotate_kernel, in_tiles),
        grid=(in_tiles + out_tiles,),
        in_specs=[
            whole,
            whole,
            pl.BlockSpec((tile, basis_in.shape[1]), lambda i: (jnp.minimum(i, in_tiles - 1), 0)),
            pl.BlockSpec((tile, basis_out.shape[1]), lambda i: (jnp.maximum(i - in_tiles, 0), 0)),
        ],
        out_specs=[result, result],
        out_shape=[shape, shape],
        compiler_params=params(24),
        cost_estimate=pl.CostEstimate(
            flops=flops, bytes_accessed=2 * basis_in.size + 2 * basis_out.size, transcendentals=0
        ),
    )(a, b, basis_in, basis_out)


def store_codes(total, in_width, store):
    side_in, side_out = total[:, :in_width], total[:, in_width:]
    level_in, level_out = level_of(side_in), level_of(side_out)
    store(0, in_width, encode(side_in, level_in))
    store(in_width, total.shape[1], encode(side_out, level_out))
    store(total.shape[1], total.shape[1] + PAD, pack_levels(level_in, level_out))


def code_kernel(in_width, *refs):
    keeps, gots, out = refs[:5], refs[5:10], refs[10]
    slot = 0
    for keep, got in zip(keeps, gots):
        for part in range(keep.shape[0] // RANK):
            rows = slice(part * RANK, (part + 1) * RANK)

            def store(lo, hi, value, slot=slot):
                out[slot, :, lo:hi] = value

            store_codes(keep[rows] + got[rows], in_width, store)
            slot += 1


def code(keeps, gots, in_width):
    width = keeps[0].shape[1]
    return pl.pallas_call(
        functools.partial(code_kernel, in_width),
        in_specs=[VMEM] * 10,
        out_specs=VMEM,
        out_shape=jax.ShapeDtypeStruct((8, RANK, width + PAD), jnp.int16),
        compiler_params=params(40),
    )(*keeps, *gots)


def resum_kernel(in_width, codes, out):
    width = codes.shape[2] - PAD
    total_in = total_out = 0.0
    for source in range(codes.shape[0]):
        unit_in, unit_out = units(codes[source, :, width:])
        total_in += as_float(codes[source, :, :in_width]) * unit_in
        total_out += as_float(codes[source, :, in_width:width]) * unit_out

    def store(lo, hi, value):
        for target in range(out.shape[0]):
            out[target, :, lo:hi] = value

    store_codes(jnp.concatenate([total_in, total_out], axis=1), in_width, store)


def resum(codes, in_width):
    return pl.pallas_call(
        functools.partial(resum_kernel, in_width),
        in_specs=[VMEM],
        out_specs=VMEM,
        out_shape=jax.ShapeDtypeStruct(codes.shape, jnp.int16),
        compiler_params=params(24),
    )(codes)


def project_kernel(own, other, acts, grads, out):
    core = core_id()
    place = lax.axis_index("inp")
    x_lo, z = place // 8, lax.rem(place, 8)
    in_width, tokens = acts.shape[1], acts.shape[0]
    width = own.shape[2] - PAD
    contract = (((1,), (1,)), ((), ()))

    def side(codes, unit, data):
        value = as_float(codes)
        high = value.astype(jnp.bfloat16)
        low = (value - high.astype(jnp.float32)).astype(jnp.bfloat16)
        data = data[...]
        got = lax.dot_general(high, data, contract, preferred_element_type=jnp.float32)
        got += lax.dot_general(low, data, contract, preferred_element_type=jnp.float32)
        return got * unit

    for codes, half in ((own, core), (other, 1 - core)):
        rows = codes.shape[0] * RANK
        unit_in, unit_out = units(codes[:, :, width:].reshape(rows, PAD))
        side_in = side(codes[:, :, :in_width].reshape(rows, in_width), unit_in, acts)
        side_out = side(codes[:, :, in_width:width].reshape(rows, width - in_width), unit_out, grads)
        level_in, level_out = level_of(side_in), level_of(side_out)
        code_in, code_out = encode(side_in, level_in), encode(side_out, level_out)
        tail = pack_levels(level_in, level_out)
        sign = 2 * half - 1
        for slot in range(8):
            away = (slot + 1) // 2
            cross = (slot + 1) % 2 if 0 < slot < 7 else half
            target = lax.rem(x_lo + cross, 2) * 8 + lax.rem(z + sign * away + 8, 8)
            span = slice(slot * RANK, (slot + 1) * RANK)
            out[target, :, 0:tokens] = code_in[span]
            out[target, :, tokens : 2 * tokens] = code_out[span]
            out[target, :, 2 * tokens :] = tail[span]


def project(own, other, acts, grads):
    tokens = acts.shape[0]
    return pl.pallas_call(
        project_kernel,
        in_specs=[VMEM] * 4,
        out_specs=VMEM,
        out_shape=jax.ShapeDtypeStruct((16, RANK, 2 * tokens + PAD), jnp.int16),
        compiler_params=params(40),
    )(own, other, acts, grads)


def score_kernel(lengths, codes, out):
    tokens = (codes.shape[2] - PAD) // 2
    side_in = side_out = 0.0
    for source in range(codes.shape[0]):
        unit_in, unit_out = units(codes[source, :, 2 * tokens :])
        side_in += as_float(codes[source, :, :tokens]) * unit_in
        side_out += as_float(codes[source, :, tokens : 2 * tokens]) * unit_out
    per_token = jnp.sum(side_in * side_out, axis=0, keepdims=True)
    position = lax.axis_index("out") * tokens + lax.broadcasted_iota(jnp.int32, (1, tokens), 1)
    lane = lax.broadcasted_iota(jnp.int32, (1, 128), 1)
    sums = jnp.zeros((1, 128), jnp.float32)
    start = jnp.int32(0)
    for example in range(lengths.shape[0]):
        finish = start + lengths[example]
        inside = (position >= start) & (position < finish)
        total = jnp.sum(jnp.where(inside, per_token, 0.0), axis=1, keepdims=True)
        sums = jnp.where(lane == example, total, sums)
        start = finish
    for target in range(out.shape[0]):
        out[target] = jnp.broadcast_to(sums, out.shape[1:])


def score(lengths, codes):
    return pl.pallas_call(
        score_kernel,
        in_specs=[SMEM, VMEM],
        out_specs=VMEM,
        out_shape=jax.ShapeDtypeStruct((16, 8, 128), jnp.float32),
        compiler_params=params(16),
    )(lengths, codes)


UP = [(x * 8 + z, x * 8 + (z + 1) % 8) for x in range(2) for z in range(8)]
DOWN = [(b, a) for a, b in UP]
ACROSS = [(i, (i + 8) % 16) for i in range(16)]
CORES = [(i, i ^ 1) for i in range(16)]
CHIPS = [[2 * chip + core for chip in range(8)] for core in range(2)]


def per_device(acts, grads, basis_in, basis_out, query_in, query_out, lengths):
    in_width = basis_in.shape[0]
    mine = jnp.concatenate([query_in.T, query_out.T], axis=1)
    other = lax.ppermute(mine, "inp", ACROSS)
    pair = jnp.concatenate([mine, other], axis=0)
    groups = [(mine, other)]
    up = down = pair
    for _ in range(3):
        up, down = lax.ppermute(up, "inp", UP), lax.ppermute(down, "inp", DOWN)
        groups.append((up, down))
    groups.append((lax.ppermute(up[:RANK], "inp", UP), lax.ppermute(down[RANK:], "inp", DOWN)))
    keeps, gots = [], []
    for a, b in groups:
        keep, send = rotate(a, b, basis_in, basis_out)
        keeps.append(keep)
        gots.append(lax.ppermute(send, "out", CORES))
    codes = code(keeps, gots, in_width)
    codes = lax.all_to_all(codes, "out", 0, 0, tiled=True, axis_index_groups=CHIPS)
    codes = resum(codes, in_width)
    own = lax.all_to_all(codes, "out", 0, 0, tiled=True, axis_index_groups=CHIPS)
    sibling = lax.ppermute(own, "out", CORES)
    sides = project(own, sibling, acts, grads)
    sides = lax.all_to_all(sides, "inp", 0, 0, tiled=True)
    sums = score(lengths, sides)
    sums = lax.all_to_all(sums, "out", 0, 0, tiled=True)
    total = jnp.sum(sums[:, 0, : lengths.shape[0]], axis=0)
    return (total / lengths.astype(jnp.float32))[:, None]


def solution(mesh):
    placed = (
        P("out", "inp"),
        P("out", "inp"),
        P("inp", "out"),
        P("inp", "out"),
        P("out", "inp"),
        P("out", "inp"),
        P(),
    )
    return jax.shard_map(
        per_device, mesh=mesh, in_specs=placed, out_specs=P(None, "inp"), check_vma=False
    )
```

time: 441 us -> 152 us (0.34)
  waiting for transfers between devices: 327 us -> 17 us
  starting transfers between devices: 0.12 us -> 27.8 us
  Pallas kernels: 0 us -> 22.5 us
  matrix products: 19.2 us -> 0 us
  between operations: 13.2 us -> 0.19 us
    psum x1 -> x0, waiting for transfers between devices: 169 us -> none  [per_device(): rotated_in, rotated_out = lax.psum((partial_in, partial_out), 'out')]
    reduce_scatter x2 -> x0, waiting for transfers between devices: 128 us -> none  [the longest x1 68.9 us: per_device(): lax.psum_scatter(output_side, 'inp', scatter_dimension=1, tiled=True)]
    all_to_all x0 -> x4, blocking collectives: none -> 79.1 us  [the longest x2 45.2 us: per_device(): lax.all_to_all(codes, 'out', 0, 0, tiled=True, axis_index_groups=CHIPS)]
    psum x1 -> x0, blocking collectives: 44.3 us -> none  [per_device(): summed = lax.psum(partial_value, 'out')]
    all_gather x1 -> x0, blocking collectives: 35.3 us -> none  [per_device(): pieces = lax.all_gather((query_in, query_out), 'inp', axis=1, tiled=True)]
    all_gather x1 -> x0, waiting for transfers between devices: 29.8 us -> none  [per_device(): pieces = lax.all_gather((query_in, query_out), 'inp', axis=1, tiled=True)]
    ppermute x0 -> x15, starting transfers between devices: none -> 27.8 us  [the longest x6 13.6 us: per_device(): up, down = (lax.ppermute(up, 'inp', UP), lax.ppermute(down, 'inp', DOWN))]
    pallas_call x0 -> x9, Pallas kernels: none -> 22.5 us  [the longest x5 18.9 us: rotate(): pl.pallas_call(functools.partial(rotate_kernel, in_tiles), grid=(in_tiles...]
  transfers between devices with their start and end apart: 4 -> 15, of which waited for: 4 -> 6; matrix products, arithmetic and copies ran while one was open for 1% -> 0% of each run, Pallas kernels for 0% -> 12%
where the time goes in v1:
time: 152 us
  blocking collectives  79.1 us (52%)
  starting transfers between devices  27.8 us (18%)
  Pallas kernels  22.5 us (15%)
  waiting for transfers between devices  17 us (11%)
  local copies, waits for them, and re-layouts  2.87 us (2%)
  other arithmetic  2.48 us (2%)
    all_to_all x2, blocking collectives, per_device(): lax.all_to_all(codes, 'out', 0, 0, tiled=True, axis_index_groups=CHIPS)  45.2 us
    all_to_all x1, blocking collectives, per_device(): sides = lax.all_to_all(sides, 'inp', 0, 0, tiled=True)  20 us
    pallas_call x5, Pallas kernels, rotate(): pl.pallas_call(functools.partial(rotate_kernel, in_tiles), grid=(in_tiles...  18.9 us
    all_to_all x1, blocking collectives, per_device(): sums = lax.all_to_all(sums, 'out', 0, 0, tiled=True)  13.9 us
    ppermute x6, starting transfers between devices, per_device(): up, down = (lax.ppermute(up, 'inp', UP), lax.ppermute(down, 'inp', DOWN))  13.6 us
    ppermute x6, waiting for transfers between devices, per_device(): up, down = (lax.ppermute(up, 'inp', UP), lax.ppermute(down, 'inp', DOWN))  8.42 us
    ppermute x5, starting transfers between devices, per_device(): gots.append(lax.ppermute(send, 'out', CORES))  6.08 us
    ppermute x1, starting transfers between devices, per_device(): lax.ppermute(down[RANK:], 'inp', DOWN)  3.05 us
  transfers between devices with their start and end apart: 15, of which 6 were waited for; matrix products, arithmetic and copies ran while one was open for 0% of the time, Pallas kernels for 12%

profile of v1, /device:TPU:1, one launch (start us, length us, event | category | flops | bytes accessed | tf_op | source)
XLA Modules:
  0.0 152.0 jit_solution(17097466283570436035)
XLA Ops:
  1.0 2.1 %collective-permute-start = (bf16[32,2304]{1,0:T(8,128)(2,1)S(1)}, bf16[32,2304]{1,0:T(8,128)(2,1)S(1)}, u32[]{:S(2)}, u32[]{:S(2)}) collective-permute-start(bf16[32,2304]{1,0:T(8,128)(2,1)S(1)} %pad_maximum_fusion.1.a_ref), channel_id=1, source_target_pairs={{0,8},{1,9},{2,10},{3,11},{4,12},{5,13},{6,14},{7,15},{8,0},{9,1},... | collective-permute-start | bytes 442376 | tf_op jit(solution)/shard_map/ppermute | solution.py:253
  3.1 2.5 %collective-permute-done.b_ref = bf16[32,2304]{1,0:T(8,128)(2,1)S(1)} collective-permute-done((bf16[32,2304]{1,0:T(8,128)(2,1)S(1)}, bf16[32,2304]{1,0:T(8,128)(2,1)S(1)}, u32[]{:S(2)}, u32[]{:S(2)}) %collective-permute-start) | collective-permute-done | bytes 147488 | tf_op jit(solution)/shard_map/ppermute | solution.py:253
  6.6 6.6 %collective-permute-start.2 = (bf16[64,2304]{1,0:T(8,128)(2,1)S(1)}, bf16[64,2304]{1,0:T(8,128)(2,1)S(1)}, u32[]{:S(2)}, u32[]{:S(2)}) collective-permute-start(bf16[64,2304]{1,0:T(8,128)(2,1)S(1)} %pad_maximum_fusion), channel_id=1, source_target_pairs={{1,0},{2,1},{3,2},{4,3},{5,4},{6,5},{7,6},{0,7},{9,8},{10,9},{11,1... | collective-permute-start | bytes 884744 | tf_op jit(solution)/shard_map/ppermute | solution.py:258
  13.2 4.8 %collective-permute-done.2.b_ref = bf16[64,2304]{1,0:T(8,128)(2,1)S(1)} collective-permute-done((bf16[64,2304]{1,0:T(8,128)(2,1)S(1)}, bf16[64,2304]{1,0:T(8,128)(2,1)S(1)}, u32[]{:S(2)}, u32[]{:S(2)}) %collective-permute-start.2) | collective-permute-done | bytes 294944 | tf_op jit(solution)/shard_map/ppermute | solution.py:258
  18.0 3.4 %collective-permute-start.4 = (bf16[64,2304]{1,0:T(8,128)(2,1)S(1)}, bf16[64,2304]{1,0:T(8,128)(2,1)S(1)}, u32[]{:S(2)}, u32[]{:S(2)}) collective-permute-start(bf16[64,2304]{1,0:T(8,128)(2,1)S(1)} %collective-permute-done.2.b_ref), channel_id=1, source_target_pairs={{1,0},{2,1},{3,2},{4,3},{5,4},{6,5},{7,6},{0,7},{9,8},{10,9},{11,1... | collective-permute-start | bytes 884744 | tf_op jit(solution)/shard_map/ppermute | solution.py:258
  21.4 3.7 %collective-permute-done.4.b_ref = bf16[64,2304]{1,0:T(8,128)(2,1)S(1)} collective-permute-done((bf16[64,2304]{1,0:T(8,128)(2,1)S(1)}, bf16[64,2304]{1,0:T(8,128)(2,1)S(1)}, u32[]{:S(2)}, u32[]{:S(2)}) %collective-permute-start.4) | collective-permute-done | bytes 294944 | tf_op jit(solution)/shard_map/ppermute | solution.py:258
  25.1 3.6 %collective-permute-start.6 = (bf16[64,2304]{1,0:T(8,128)(2,1)S(1)}, bf16[64,2304]{1,0:T(8,128)(2,1)S(1)}, u32[]{:S(2)}, u32[]{:S(2)}) collective-permute-start(bf16[64,2304]{1,0:T(8,128)(2,1)S(1)} %collective-permute-done.4.b_ref), channel_id=1, source_target_pairs={{1,0},{2,1},{3,2},{4,3},{5,4},{6,5},{7,6},{0,7},{9,8},{10,9},{11,1... | collective-permute-start | bytes 884744 | tf_op jit(solution)/shard_map/ppermute | solution.py:258
  28.7 2.8 %copy-done = bf16[1792,1792]{1,0:T(8,128)(2,1)S(1)} copy-done((bf16[1792,1792]{1,0:T(8,128)(2,1)S(1)}, bf16[1792,1792]{1,0:T(8,128)(2,1)}, u32[]{:S(2)}) %copy-start) | copy-done | bytes 6422552
  31.5 3.9 %shard_map.74 = (f32[64,2304]{1,0:T(8,128)S(1)}, f32[64,2304]{1,0:T(8,128)S(1)}) custom-call(bf16[64,2304]{1,0:T(8,128)(2,1)S(1)} %collective-permute-done.1.a_ref, bf16[64,2304]{1,0:T(8,128)(2,1)S(1)} %collective-permute-done.2.b_ref, bf16[1792,1792]{1,0:T(8,128)(2,1)S(1)} %copy-done, bf16[512,512]{1,0:T(8,128)(2,1)S(1)} %copy-done.1), custom_call_target="tpu_custom_call" | custom-call | flops 889192448 | bytes 6946816 | tf_op jit(solution)/shard_map/pallas_call | solution.py:88
  35.4 3.7 %collective-permute-start.10 = (f32[64,2304]{1,0:T(8,128)S(1)}, f32[64,2304]{1,0:T(8,128)S(1)}, u32[]{:S(2)}, u32[]{:S(2)}) collective-permute-start(f32[64,2304]{1,0:T(8,128)S(1)} %get-tuple-element.21), channel_id=1, source_target_pairs={{0,16},{16,0},{32,48},{48,32},{64,80},{80,64},{96,112},{112,96},{1... | collective-permute-start | bytes 1769480 | tf_op jit(solution)/shard_map/ppermute | solution.py:265
  39.1 3.9 %shard_map.75 = (f32[64,2304]{1,0:T(8,128)S(1)}, f32[64,2304]{1,0:T(8,128)S(1)}) custom-call(bf16[64,2304]{1,0:T(8,128)(2,1)S(1)} %collective-permute-done.3.a_ref, bf16[64,2304]{1,0:T(8,128)(2,1)S(1)} %collective-permute-done.4.b_ref, bf16[1792,1792]{1,0:T(8,128)(2,1)S(1)} %copy-done, bf16[512,512]{1,0:T(8,128)(2,1)S(1)} %copy-done.1), custom_call_target="tpu_custom_call" | custom-call | flops 889192448 | bytes 6946816 | tf_op jit(solution)/shard_map/pallas_call | solution.py:88
  43.2 3.9 %shard_map.76 = (f32[64,2304]{1,0:T(8,128)S(1)}, f32[64,2304]{1,0:T(8,128)S(1)}) custom-call(bf16[64,2304]{1,0:T(8,128)(2,1)S(1)} %collective-permute-done.5.a_ref, bf16[64,2304]{1,0:T(8,128)(2,1)S(1)} %collective-permute-done.6.b_ref, bf16[1792,1792]{1,0:T(8,128)(2,1)S(1)} %copy-done, bf16[512,512]{1,0:T(8,128)(2,1)S(1)} %copy-done.1), custom_call_target="tpu_custom_call" | custom-call | flops 889192448 | bytes 6946816 | tf_op jit(solution)/shard_map/pallas_call | solution.py:88
  47.7 3.1 %collective-permute-start.8 = (bf16[32,2304]{1,0:T(8,128)(2,1)S(1)}, bf16[32,2304]{1,0:T(8,128)(2,1)S(1)}, u32[]{:S(2)}, u32[]{:S(2)}) collective-permute-start(bf16[32,2304]{1,0:T(8,128)(2,1)S(1)} %slice.13), channel_id=1, source_target_pairs={{1,0},{2,1},{3,2},{4,3},{5,4},{6,5},{7,6},{0,7},{9,8},{10,9},{11,1... | collective-permute-start | bytes 442376 | tf_op jit(solution)/shard_map/ppermute | solution.py:260
  50.9 3.6 %shard_map.73 = (f32[32,2304]{1,0:T(8,128)S(1)}, f32[32,2304]{1,0:T(8,128)S(1)}) custom-call(bf16[32,2304]{1,0:T(8,128)(2,1)S(1)} %pad_maximum_fusion.1.a_ref, bf16[32,2304]{1,0:T(8,128)(2,1)S(1)} %collective-permute-done.b_ref, bf16[1792,1792]{1,0:T(8,128)(2,1)S(1)} %bitcast.5, bf16[512,512]{1,0:T(8,128)(2,1)S(1)} %copy-done.1), custom_call_target="tpu_custom_call" | custom-call | flops 444596224 | bytes 6946816 | tf_op jit(solution)/shard_map/pallas_call | solution.py:88
  54.9 2.2 %collective-permute-done.7.a_ref = bf16[32,2304]{1,0:T(8,128)(2,1)S(1)} collective-permute-done((bf16[32,2304]{1,0:T(8,128)(2,1)S(1)}, bf16[32,2304]{1,0:T(8,128)(2,1)S(1)}, u32[]{:S(2)}, u32[]{:S(2)}) %collective-permute-start.7) | collective-permute-done | bytes 147488 | tf_op jit(solution)/shard_map/ppermute | solution.py:260
  57.1 3.6 %shard_map.77 = (f32[32,2304]{1,0:T(8,128)S(1)}, f32[32,2304]{1,0:T(8,128)S(1)}) custom-call(bf16[32,2304]{1,0:T(8,128)(2,1)S(1)} %collective-permute-done.7.a_ref, bf16[32,2304]{1,0:T(8,128)(2,1)S(1)} %collective-permute-done.8.b_ref, bf16[1792,1792]{1,0:T(8,128)(2,1)S(1)} %bitcast.5, bf16[512,512]{1,0:T(8,128)(2,1)S(1)} %copy-done.1), custom_call_target="tpu_custom_call" | custom-call | flops 444596224 | bytes 6946816 | tf_op jit(solution)/shard_map/pallas_call | solution.py:88
  60.7 1.2 collective-permute-start.13
  63.8 25.2 %all_to_all.20.codes = s16[8,32,2432]{2,1,0:T(8,128)(2,1)S(1)} all-to-all(s16[8,32,2432]{2,1,0:T(8,128)(2,1)S(1)} %shard_map.78), channel_id=1, replica_groups={{0,32,64,96,128,160,192,224},{16,48,80,112,144,176,208,240},{1,33,65,97..., dimensions={0} | all-to-all | bytes 2490368 | tf_op jit(solution)/shard_map/all_to_all | solution.py:267
  89.4 20.0 %all_to_all.21.own = s16[8,32,2432]{2,1,0:T(8,128)(2,1)S(1)} all-to-all(s16[8,32,2432]{2,1,0:T(8,128)(2,1)S(1)} %shard_map.79), channel_id=1, replica_groups={{0,32,64,96,128,160,192,224},{16,48,80,112,144,176,208,240},{1,33,65,97..., dimensions={0} | all-to-all | bytes 2490368 | tf_op jit(solution)/shard_map/all_to_all | solution.py:269
  109.4 2.9 %collective-permute-start.14 = (s16[8,32,2432]{2,1,0:T(8,128)(2,1)S(1)}, s16[8,32,2432]{2,1,0:T(8,128)(2,1)S(1)}, u32[]{:S(2)}, u32[]{:S(2)}) collective-permute-start(s16[8,32,2432]{2,1,0:T(8,128)(2,1)S(1)} %all_to_all.21.own), channel_id=1, source_target_pairs={{0,16},{16,0},{32,48},{48,32},{64,80},{80,64},{96,112},{112,96},{1... | collective-permute-start | bytes 3735560 | tf_op jit(solution)/shard_map/ppermute | solution.py:270
  112.3 2.6 %collective-permute-done.14.other = s16[8,32,2432]{2,1,0:T(8,128)(2,1)S(1)} collective-permute-done((s16[8,32,2432]{2,1,0:T(8,128)(2,1)S(1)}, s16[8,32,2432]{2,1,0:T(8,128)(2,1)S(1)}, u32[]{:S(2)}, u32[]{:S(2)}) %collective-permute-start.14) | collective-permute-done | bytes 1245216 | tf_op jit(solution)/shard_map/ppermute | solution.py:270
  114.9 1.7 %shard_map.80 = s16[16,32,640]{2,1,0:T(8,128)(2,1)S(1)} custom-call(s16[8,32,2432]{2,1,0:T(8,128)(2,1)S(1)} %all_to_all.21.own, s16[8,32,2432]{2,1,0:T(8,128)(2,1)S(1)} %collective-permute-done.14.other, bf16[256,1792]{1,0:T(8,128)(2,1)S(1)} %copy-done.2, bf16[256,512]{1,0:T(8,128)(2,1)S(1)} %copy-done.3), custom_call_target="tpu_custom_call" | custom-call | tf_op jit(solution)/shard_map/pallas_call | solution.py:202
  116.5 20.0 %all_to_all.22.codes = s16[16,32,640]{2,1,0:T(8,128)(2,1)S(1)} all-to-all(s16[16,32,640]{2,1,0:T(8,128)(2,1)S(1)} %shard_map.80), channel_id=1, replica_groups=mesh['out'=16,'inp'=16] {'inp'}, dimensions={0} | all-to-all | bytes 1310720 | tf_op jit(solution)/shard_map/all_to_all | solution.py:272
  137.5 13.9 %all_to_all.23 = f32[16,8,128]{2,1,0:T(8,128)S(1)} all-to-all(f32[16,8,128]{2,1,0:T(8,128)S(1)} %shard_map.81), channel_id=1, replica_groups=mesh['out'=16,'inp'=16] {'out'}, dimensions={0} | all-to-all | bytes 131072 | tf_op jit(solution)/shard_map/all_to_all | solution.py:274
  (40 shorter events, 6.9 us)
Async XLA Ops:
  0.0 28.6 %copy-start.1 = (bf16[512,512]{1,0:T(8,128)(2,1)S(1)}, bf16[512,512]{1,0:T(8,128)(2,1)}, u32[]{:S(2)}) copy-start(bf16[512,512]{1,0:T(8,128)(2,1)} %basis_out.9) | copy-start | bytes 1572868
  1.0 4.7 %collective-permute-start = (bf16[32,2304]{1,0:T(8,128)(2,1)S(1)}, bf16[32,2304]{1,0:T(8,128)(2,1)S(1)}, u32[]{:S(2)}, u32[]{:S(2)}) collective-permute-start(bf16[32,2304]{1,0:T(8,128)(2,1)S(1)} %pad_maximum_fusion.1.a_ref), channel_id=1, source_target_pairs={{0,8},{1,9},{2,10},{3,11},{4,12},{5,13},{6,14},{7,15},{8,0},{9,1},... | collective-permute-start | bytes 442376 | tf_op jit(solution)/shard_map/ppermute | solution.py:253
  6.6 11.4 %collective-permute-start.2 = (bf16[64,2304]{1,0:T(8,128)(2,1)S(1)}, bf16[64,2304]{1,0:T(8,128)(2,1)S(1)}, u32[]{:S(2)}, u32[]{:S(2)}) collective-permute-start(bf16[64,2304]{1,0:T(8,128)(2,1)S(1)} %pad_maximum_fusion), channel_id=1, source_target_pairs={{1,0},{2,1},{3,2},{4,3},{5,4},{6,5},{7,6},{0,7},{9,8},{10,9},{11,1... | collective-permute-start | bytes 884744 | tf_op jit(solution)/shard_map/ppermute | solution.py:258
  13.2 8.2 %collective-permute-start.1 = (bf16[64,2304]{1,0:T(8,128)(2,1)S(1)}, bf16[64,2304]{1,0:T(8,128)(2,1)S(1)}, u32[]{:S(2)}, u32[]{:S(2)}) collective-permute-start(bf16[64,2304]{1,0:T(8,128)(2,1)S(1)} %pad_maximum_fusion), channel_id=1, source_target_pairs={{0,1},{1,2},{2,3},{3,4},{4,5},{5,6},{6,7},{7,0},{8,9},{9,10},{10,1... | collective-permute-start | bytes 884744 | tf_op jit(solution)/shard_map/ppermute | solution.py:258
  18.0 7.1 %collective-permute-start.4 = (bf16[64,2304]{1,0:T(8,128)(2,1)S(1)}, bf16[64,2304]{1,0:T(8,128)(2,1)S(1)}, u32[]{:S(2)}, u32[]{:S(2)}) collective-permute-start(bf16[64,2304]{1,0:T(8,128)(2,1)S(1)} %collective-permute-done.2.b_ref), channel_id=1, source_target_pairs={{1,0},{2,1},{3,2},{4,3},{5,4},{6,5},{7,6},{0,7},{9,8},{10,9},{11,1... | collective-permute-start | bytes 884744 | tf_op jit(solution)/shard_map/ppermute | solution.py:258
  21.4 7.2 %collective-permute-start.3 = (bf16[64,2304]{1,0:T(8,128)(2,1)S(1)}, bf16[64,2304]{1,0:T(8,128)(2,1)S(1)}, u32[]{:S(2)}, u32[]{:S(2)}) collective-permute-start(bf16[64,2304]{1,0:T(8,128)(2,1)S(1)} %collective-permute-done.1.a_ref), channel_id=1, source_target_pairs={{0,1},{1,2},{2,3},{3,4},{4,5},{5,6},{6,7},{7,0},{8,9},{9,10},{10,1... | collective-permute-start | bytes 884744 | tf_op jit(solution)/shard_map/ppermute | solution.py:258
  25.1 18.2 %collective-permute-start.6 = (bf16[64,2304]{1,0:T(8,128)(2,1)S(1)}, bf16[64,2304]{1,0:T(8,128)(2,1)S(1)}, u32[]{:S(2)}, u32[]{:S(2)}) collective-permute-start(bf16[64,2304]{1,0:T(8,128)(2,1)S(1)} %collective-permute-done.4.b_ref), channel_id=1, source_target_pairs={{1,0},{2,1},{3,2},{4,3},{5,4},{6,5},{7,6},{0,7},{9,8},{10,9},{11,1... | collective-permute-start | bytes 884744 | tf_op jit(solution)/shard_map/ppermute | solution.py:258
  28.6 14.6 %collective-permute-start.5 = (bf16[64,2304]{1,0:T(8,128)(2,1)S(1)}, bf16[64,2304]{1,0:T(8,128)(2,1)S(1)}, u32[]{:S(2)}, u32[]{:S(2)}) collective-permute-start(bf16[64,2304]{1,0:T(8,128)(2,1)S(1)} %collective-permute-done.3.a_ref), channel_id=1, source_target_pairs={{0,1},{1,2},{2,3},{3,4},{4,5},{5,6},{6,7},{7,0},{8,9},{9,10},{10,1... | collective-permute-start | bytes 884744 | tf_op jit(solution)/shard_map/ppermute | solution.py:258
  28.6 2.8 %copy-start = (bf16[1792,1792]{1,0:T(8,128)(2,1)S(1)}, bf16[1792,1792]{1,0:T(8,128)(2,1)}, u32[]{:S(2)}) copy-start(bf16[1792,1792]{1,0:T(8,128)(2,1)} %basis_in.9) | copy-start | bytes 19267588
  35.4 26.6 %collective-permute-start.10 = (f32[64,2304]{1,0:T(8,128)S(1)}, f32[64,2304]{1,0:T(8,128)S(1)}, u32[]{:S(2)}, u32[]{:S(2)}) collective-permute-start(f32[64,2304]{1,0:T(8,128)S(1)} %get-tuple-element.21), channel_id=1, source_target_pairs={{0,16},{16,0},{32,48},{48,32},{64,80},{80,64},{96,112},{112,96},{1... | collective-permute-start | bytes 1769480 | tf_op jit(solution)/shard_map/ppermute | solution.py:265
  39.1 11.7 %slice-start = ((s8[6422528]{0:T(1024)(128)(4,1)}), s8[4194304]{0:T(1024)(128)(4,1)S(1)}, s32[]{:S(2)}) async-start(s8[6422528]{0:T(1024)(128)(4,1)} %bitcast.4), calls=%async_computation.4 | async-start | bytes 8388608
  43.1 7.8 %slice-start.1 = ((s8[6422528]{0:T(1024)(128)(4,1)}), s8[2228224]{0:T(1024)(128)(4,1)S(1)}, s32[]{:S(2)}) async-start(s8[6422528]{0:T(1024)(128)(4,1)} %bitcast.4), calls=%async_computation.5 | async-start | bytes 4456448
  43.1 18.9 %collective-permute-start.11 = (f32[64,2304]{1,0:T(8,128)S(1)}, f32[64,2304]{1,0:T(8,128)S(1)}, u32[]{:S(2)}, u32[]{:S(2)}) collective-permute-start(f32[64,2304]{1,0:T(8,128)S(1)} %get-tuple-element.22), channel_id=1, source_target_pairs={{0,16},{16,0},{32,48},{48,32},{64,80},{80,64},{96,112},{112,96},{1... | collective-permute-start | bytes 1769480 | tf_op jit(solution)/shard_map/ppermute | solution.py:265
  47.1 16.0 %collective-permute-start.12 = (f32[64,2304]{1,0:T(8,128)S(1)}, f32[64,2304]{1,0:T(8,128)S(1)}, u32[]{:S(2)}, u32[]{:S(2)}) collective-permute-start(f32[64,2304]{1,0:T(8,128)S(1)} %get-tuple-element.23), channel_id=1, source_target_pairs={{0,16},{16,0},{32,48},{48,32},{64,80},{80,64},{96,112},{112,96},{1... | collective-permute-start | bytes 1769480 | tf_op jit(solution)/shard_map/ppermute | solution.py:265
  47.7 6.8 %collective-permute-start.8 = (bf16[32,2304]{1,0:T(8,128)(2,1)S(1)}, bf16[32,2304]{1,0:T(8,128)(2,1)S(1)}, u32[]{:S(2)}, u32[]{:S(2)}) collective-permute-start(bf16[32,2304]{1,0:T(8,128)(2,1)S(1)} %slice.13), channel_id=1, source_target_pairs={{1,0},{2,1},{3,2},{4,3},{5,4},{6,5},{7,6},{0,7},{9,8},{10,9},{11,1... | collective-permute-start | bytes 442376 | tf_op jit(solution)/shard_map/ppermute | solution.py:260
  50.8 6.4 %collective-permute-start.7 = (bf16[32,2304]{1,0:T(8,128)(2,1)S(1)}, bf16[32,2304]{1,0:T(8,128)(2,1)S(1)}, u32[]{:S(2)}, u32[]{:S(2)}) collective-permute-start(bf16[32,2304]{1,0:T(8,128)(2,1)S(1)} %slice.12), channel_id=1, source_target_pairs={{0,1},{1,2},{2,3},{3,4},{4,5},{5,6},{6,7},{7,0},{8,9},{9,10},{10,1... | collective-permute-start | bytes 442376 | tf_op jit(solution)/shard_map/ppermute | solution.py:260
  54.5 7.5 %collective-permute-start.9 = (f32[32,2304]{1,0:T(8,128)S(1)}, f32[32,2304]{1,0:T(8,128)S(1)}, u32[]{:S(2)}, u32[]{:S(2)}) collective-permute-start(f32[32,2304]{1,0:T(8,128)S(1)} %get-tuple-element.20), channel_id=1, source_target_pairs={{0,16},{16,0},{32,48},{48,32},{64,80},{80,64},{96,112},{112,96},{1... | collective-permute-start | bytes 884744 | tf_op jit(solution)/shard_map/ppermute | solution.py:265
  60.7 2.5 %collective-permute-start.13 = (f32[32,2304]{1,0:T(8,128)S(1)}, f32[32,2304]{1,0:T(8,128)S(1)}, u32[]{:S(2)}, u32[]{:S(2)}) collective-permute-start(f32[32,2304]{1,0:T(8,128)S(1)} %get-tuple-element.24), channel_id=1, source_target_pairs={{0,16},{16,0},{32,48},{48,32},{64,80},{80,64},{96,112},{112,96},{1... | collective-permute-start | bytes 884744 | tf_op jit(solution)/shard_map/ppermute | solution.py:265
  89.4 25.5 %copy-start.2 = (bf16[256,1792]{1,0:T(8,128)(2,1)S(1)}, bf16[256,1792]{1,0:T(8,128)(2,1)}, u32[]{:S(2)}) copy-start(bf16[256,1792]{1,0:T(8,128)(2,1)} %acts.1) | copy-start | bytes 2752516
  89.4 25.5 %copy-start.3 = (bf16[256,512]{1,0:T(8,128)(2,1)S(1)}, bf16[256,512]{1,0:T(8,128)(2,1)}, u32[]{:S(2)}) copy-start(bf16[256,512]{1,0:T(8,128)(2,1)} %grads.1) | copy-start | bytes 786436
  109.4 5.4 %collective-permute-start.14 = (s16[8,32,2432]{2,1,0:T(8,128)(2,1)S(1)}, s16[8,32,2432]{2,1,0:T(8,128)(2,1)S(1)}, u32[]{:S(2)}, u32[]{:S(2)}) collective-permute-start(s16[8,32,2432]{2,1,0:T(8,128)(2,1)S(1)} %all_to_all.21.own), channel_id=1, source_target_pairs={{0,16},{16,0},{32,48},{48,32},{64,80},{80,64},{96,112},{112,96},{1... | collective-permute-start | bytes 3735560 | tf_op jit(solution)/shard_map/ppermute | solution.py:270
  116.5 20.0 %copy-start.4 = (s32[16]{0:T(128)S(1)}, s32[16]{0:T(128)}, u32[]{:S(2)}) copy-start(s32[16]{0:T(128)} %lengths.1) | copy-start | bytes 196

commit v2 on v1

--- a/solution.py
+++ b/solution.py
@@ -13,6 +13,7 @@
 PAD = 128
 VMEM = pl.BlockSpec(memory_space=pltpu.VMEM)
 SMEM = pl.BlockSpec(memory_space=pltpu.SMEM)
+BRIEF = pl.CostEstimate(flops=100_000_000, bytes_accessed=100_000, transcendentals=0)
 
 
 def params(mib):
@@ -54,53 +55,73 @@
     return unit_of(tail[:, 0:1]), unit_of(tail[:, PAD // 2 : PAD // 2 + 1])
 
 
-def rotate_kernel(in_tiles, a_ref, b_ref, basis_in, basis_out, keep, send):
-    step = pl.program_id(0)
-    first = core_id() == 0
+def stage_kernel(basis_in, basis_out, out_in, out_out, sems):
+    copies = [
+        pltpu.make_async_copy(basis_in, out_in, sems.at[0]),
+        pltpu.make_async_copy(basis_out, out_out, sems.at[1]),
+    ]
+    for copy in copies:
+        copy.start()
+    for copy in copies:
+        copy.wait()
+
+
+def stage(basis_in, basis_out):
+    return pl.pallas_call(
+        stage_kernel,
+        in_specs=[pl.BlockSpec(memory_space=pltpu.HBM)] * 2,
+        out_specs=[VMEM] * 2,
+        out_shape=[pltpu.VMEM(x.shape, x.dtype) for x in (basis_in, basis_out)],
+        scratch_shapes=[pltpu.SemaphoreType.DMA((2,))],
+        compiler_params=params(16),
+        cost_estimate=BRIEF,
+    )(basis_in, basis_out)
+
+
+def rotate_kernel(count, *refs):
+    firsts, seconds = refs[:count], refs[count : 2 * count]
+    basis_in, basis_out, keep, send, rows = refs[2 * count :]
+    own = core_id() == 0
+    half = keep.shape[0]
+    lo = 0
+    for first, second in zip(firsts, seconds):
+        a, b = first[...], second[...]
+        hi = lo + a.shape[0]
+        rows[lo:hi] = jnp.where(own, a, b)
+        rows[half + lo : half + hi] = jnp.where(own, b, a)
+        lo = hi
     width = basis_in.shape[1]
-    contract = (((1,), (1,)), ((), ()))
-
-    def run(lo, hi, basis):
-        a, b = a_ref[:, lo:hi], b_ref[:, lo:hi]
-        rows = jnp.concatenate([jnp.where(first, a, b), jnp.where(first, b, a)], axis=0)
-        got = lax.dot_general(rows, basis[...], contract, preferred_element_type=jnp.float32)
-        half = a.shape[0]
-        keep[...] = got[:half]
-        send[...] = got[half:]
-
-    @pl.when(step < in_tiles)
-    def _():
-        run(0, width, basis_in)
-
-    @pl.when(step >= in_tiles)
-    def _():
-        run(width, width + basis_out.shape[1], basis_out)
-
-
-def rotate(a, b, basis_in, basis_out):
     tile = 256
-    rows, width = a.shape
-    in_tiles, out_tiles = basis_in.shape[0] // tile, basis_out.shape[0] // tile
-    whole = pl.BlockSpec((rows, width), lambda i: (0, 0))
-    result = pl.BlockSpec((rows, tile), lambda i: (0, i))
-    shape = jax.ShapeDtypeStruct((rows, width), jnp.float32)
-    flops = 4 * rows * (basis_in.size + basis_out.size)
-    return pl.pallas_call(
-        functools.partial(rotate_kernel, in_tiles),
-        grid=(in_tiles + out_tiles,),
-        in_specs=[
-            whole,
-            whole,
-            pl.BlockSpec((tile, basis_in.shape[1]), lambda i: (jnp.minimum(i, in_tiles - 1), 0)),
-            pl.BlockSpec((tile, basis_out.shape[1]), lambda i: (jnp.maximum(i - in_tiles, 0), 0)),
-        ],
-        out_specs=[result, result],
+    for basis, base in ((basis_in, 0), (basis_out, width)):
+        columns = slice(base, base + basis.shape[1])
+        for lo in range(0, basis.shape[0], tile):
+            got = lax.dot_general(
+                rows[:, columns],
+                basis[lo : lo + tile],
+                (((1,), (1,)), ((), ())),
+                preferred_element_type=jnp.float32,
+            )
+            keep[:, base + lo : base + lo + tile] = got[:half]
+            send[:, base + lo : base + lo + tile] = got[half:]
+
+
+def rotate(firsts, seconds, basis_in, basis_out):
+    count = len(firsts)
+    half, width = sum(x.shape[0] for x in firsts), firsts[0].shape[1]
+    shape = jax.ShapeDtypeStruct((half, width), jnp.float32)
+    return pl.pallas_call(
+        functools.partial(rotate_kernel, count),
+        in_specs=[VMEM] * (2 * count + 2),
+        out_specs=[VMEM] * 2,
         out_shape=[shape, shape],
-        compiler_params=params(24),
+        scratch_shapes=[pltpu.VMEM((2 * half, width), jnp.bfloat16)],
+        compiler_params=params(16),
         cost_estimate=pl.CostEstimate(
-            flops=flops, bytes_accessed=2 * basis_in.size + 2 * basis_out.size, transcendentals=0
+            flops=4 * half * (basis_in.size + basis_out.size),
+            bytes_accessed=100_000,
+            transcendentals=0,
         ),
-    )(a, b, basis_in, basis_out)
+    )(*firsts, *seconds, basis_in, basis_out)
 
 
 def store_codes(total, in_width, store):
@@ -111,29 +132,31 @@
     store(total.shape[1], total.shape[1] + PAD, pack_levels(level_in, level_out))
 
 
-def code_kernel(in_width, *refs):
-    keeps, gots, out = refs[:5], refs[5:10], refs[10]
+def code_kernel(in_width, keep, got, *refs):
+    done, out = refs[:-1], refs[-1]
     slot = 0
-    for keep, got in zip(keeps, gots):
-        for part in range(keep.shape[0] // RANK):
-            rows = slice(part * RANK, (part + 1) * RANK)
-
-            def store(lo, hi, value, slot=slot):
-                out[slot, :, lo:hi] = value
-
-            store_codes(keep[rows] + got[rows], in_width, store)
-            slot += 1
-
-
-def code(keeps, gots, in_width):
-    width = keeps[0].shape[1]
+    for codes in done:
+        out[slot : slot + codes.shape[0]] = codes[...]
+        slot += codes.shape[0]
+    for part in range(keep.shape[0] // RANK):
+        rows = slice(part * RANK, (part + 1) * RANK)
+
+        def store(lo, hi, value, slot=slot + part):
+            out[slot, :, lo:hi] = value
+
+        store_codes(keep[rows] + got[rows], in_width, store)
+
+
+def code(keep, got, in_width, *done):
+    slots = keep.shape[0] // RANK + sum(codes.shape[0] for codes in done)
     return pl.pallas_call(
         functools.partial(code_kernel, in_width),
-        in_specs=[VMEM] * 10,
+        in_specs=[VMEM] * (2 + len(done)),
         out_specs=VMEM,
-        out_shape=jax.ShapeDtypeStruct((8, RANK, width + PAD), jnp.int16),
-        compiler_params=params(40),
-    )(*keeps, *gots)
+        out_shape=jax.ShapeDtypeStruct((slots, RANK, keep.shape[1] + PAD), jnp.int16),
+        compiler_params=params(16),
+        cost_estimate=BRIEF,
+    )(keep, got, *done)
 
 
 def resum_kernel(in_width, codes, out):
@@ -251,19 +274,37 @@
     in_width = basis_in.shape[0]
     mine = jnp.concatenate([query_in.T, query_out.T], axis=1)
     other = lax.ppermute(mine, "inp", ACROSS)
-    pair = jnp.concatenate([mine, other], axis=0)
-    groups = [(mine, other)]
-    up = down = pair
-    for _ in range(3):
-        up, down = lax.ppermute(up, "inp", UP), lax.ppermute(down, "inp", DOWN)
-        groups.append((up, down))
-    groups.append((lax.ppermute(up[:RANK], "inp", UP), lax.ppermute(down[RANK:], "inp", DOWN)))
-    keeps, gots = [], []
-    for a, b in groups:
-        keep, send = rotate(a, b, basis_in, basis_out)
-        keeps.append(keep)
-        gots.append(lax.ppermute(send, "out", CORES))
-    codes = code(keeps, gots, in_width)
+    other, basis_in, basis_out = lax.optimization_barrier(
+        (other, *stage(basis_in, basis_out))
+    )
+    basis_in = pltpu.with_memory_space_constraint(basis_in, pltpu.VMEM)
+    basis_out = pltpu.with_memory_space_constraint(basis_out, pltpu.VMEM)
+
+
+    def hop(ends):
+        up, down = ends
+        return lax.ppermute(up, "inp", UP), lax.ppermute(down, "inp", DOWN)
+
+    def rotated(*ends):
+        firsts, seconds = zip(*ends)
+        return rotate(firsts, seconds, basis_in, basis_out)
+
+    def finish(rotated, *done):
+        keep, send = rotated
+        return code(keep, lax.ppermute(send, "out", CORES), in_width, *done)
+
+    a1 = hop((mine, mine))
+    b1 = hop((other, other))
+    a2 = hop(a1)
+    b2 = hop(b1)
+    a3 = hop(a2)
+    b3 = hop(b2)
+    a4 = lax.ppermute(a3[0], "inp", UP)
+    b4 = lax.ppermute(b3[1], "inp", DOWN)
+    keep, send = rotated((mine, other), a1, b1, a2, b2, a3, b3)
+    send, a4, b4 = lax.optimization_barrier((send, a4, b4))
+    end = rotated((a4, b4))
+    codes = finish(end, finish((keep, send)))
     codes = lax.all_to_all(codes, "out", 0, 0, tiled=True, axis_index_groups=CHIPS)
     codes = resum(codes, in_width)
     own = lax.all_to_all(codes, "out", 0, 0, tiled=True, axis_index_groups=CHIPS)

time: 152 us -> 138 us (0.908)
  Pallas kernels: 22.5 us -> 9.98 us
  waiting for transfers between devices: 17 us -> 7.19 us
  starting transfers between devices: 27.8 us -> 33.5 us
  blocking collectives: 79.1 us -> 81.1 us
    pallas_call x5 -> x3, Pallas kernels: 18.9 us -> 6.23 us  [the longest x2 5.58 us: rotate(): pl.pallas_call(functools.partial(rotate_kernel, count), in_specs=[VMEM] *...]
    ppermute x13 -> x16, waiting for transfers between devices: 11.9 us -> 4.62 us  [the longest x12 3.2 us: hop(): return (lax.ppermute(up, 'inp', UP), lax.ppermute(down, 'inp', DOWN))]
    ppermute x13 -> x16, starting transfers between devices: 22.8 us -> 28.5 us  [the longest x12 19.7 us: hop(): return (lax.ppermute(up, 'inp', UP), lax.ppermute(down, 'inp', DOWN))]
    all_to_all x1, blocking collectives: 20 us -> 22.6 us  [per_device(): sides = lax.all_to_all(sides, 'inp', 0, 0, tiled=True)]
    ppermute x1, waiting for transfers between devices: 2.53 us -> 0.01 us  [per_device(): other = lax.ppermute(mine, 'inp', ACROSS)]
    unnamed x14 -> x10, local copies, waits for them, and re-layouts: 2.85 us -> 3.88 us
  transfers between devices with their start and end apart: 15 -> 18, of which waited for: 6 -> 6; matrix products, arithmetic and copies ran while one was open for 0% -> 0% of each run, Pallas kernels for 12% -> 5%
where the time goes in v2:
time: 138 us; the launch traced here: 137 us
  blocking collectives  81.1 us (59%)
  starting transfers between devices  33.5 us (24%)
  Pallas kernels  9.98 us (7%)
  waiting for transfers between devices  7.19 us (5%)
  local copies, waits for them, and re-layouts  3.88 us (3%)
  other arithmetic  1.48 us (1%)
    all_to_all x2, blocking collectives, per_device(): lax.all_to_all(codes, 'out', 0, 0, tiled=True, axis_index_groups=CHIPS)  44.9 us
    all_to_all x1, blocking collectives, per_device(): sides = lax.all_to_all(sides, 'inp', 0, 0, tiled=True)  22.6 us
    ppermute x12, starting transfers between devices, hop(): return (lax.ppermute(up, 'inp', UP), lax.ppermute(down, 'inp', DOWN))  19.7 us
    all_to_all x1, blocking collectives, per_device(): sums = lax.all_to_all(sums, 'out', 0, 0, tiled=True)  13.6 us
    pallas_call x2, Pallas kernels, rotate(): pl.pallas_call(functools.partial(rotate_kernel, count), in_specs=[VMEM] *...  5.58 us
    ppermute x2, starting transfers between devices, finish(): return code(keep, lax.ppermute(send, 'out', CORES), in_width, *done)  5.55 us
    unnamed x10, local copies, waits for them, and re-layouts  3.88 us
    ppermute x1, starting transfers between devices, per_device(): b4 = lax.ppermute(b3[1], 'inp', DOWN)  3.21 us
  transfers between devices with their start and end apart: 18, of which 6 were waited for; matrix products, arithmetic and copies ran while one was open for 0% of the time, Pallas kernels for 5%

profile of v2, /device:TPU:1, one launch (start us, length us, event | category | flops | bytes accessed | tf_op | source)
XLA Modules:
  0.0 137.2 jit_solution(551119328155963337)
XLA Ops:
  0.0 0.9 pad_maximum_fusion.refs_0_
  0.9 2.1 %collective-permute-start.1 = (bf16[32,2304]{1,0:T(8,128)(2,1)S(1)}, bf16[32,2304]{1,0:T(8,128)(2,1)S(1)}, u32[]{:S(2)}, u32[]{:S(2)}) collective-permute-start(bf16[32,2304]{1,0:T(8,128)(2,1)S(1)} %pad_maximum_fusion.refs_0_), channel_id=1, source_target_pairs={{0,8},{1,9},{2,10},{3,11},{4,12},{5,13},{6,14},{7,15},{8,0},{9,1},... | collective-permute-start | bytes 442376 | tf_op jit(solution)/shard_map/ppermute | solution.py:276
  3.1 1.6 %collective-permute-start = (bf16[32,2304]{1,0:T(8,128)(2,1)S(1)}, bf16[32,2304]{1,0:T(8,128)(2,1)S(1)}, u32[]{:S(2)}, u32[]{:S(2)}) collective-permute-start(bf16[32,2304]{1,0:T(8,128)(2,1)S(1)} %pad_maximum_fusion.refs_0_), channel_id=1, source_target_pairs={{0,1},{1,2},{2,3},{3,4},{4,5},{5,6},{6,7},{7,0},{8,9},{9,10},{10,1... | collective-permute-start | bytes 442376 | tf_op jit(solution)/shard_map/ppermute | solution.py:286
  4.7 2.8 %copy-done = bf16[1792,1792]{1,0:T(8,128)(2,1)S(1)} copy-done((bf16[1792,1792]{1,0:T(8,128)(2,1)S(1)}, bf16[1792,1792]{1,0:T(8,128)(2,1)}, u32[]{:S(2)}) %copy-start) | copy-done | bytes 6422552
  7.5 1.0 copy-done.2
  9.2 4.0 %collective-permute-start.8 = (bf16[32,2304]{1,0:T(8,128)(2,1)S(1)}, bf16[32,2304]{1,0:T(8,128)(2,1)S(1)}, u32[]{:S(2)}, u32[]{:S(2)}) collective-permute-start(bf16[32,2304]{1,0:T(8,128)(2,1)S(1)} %collective-permute-done.1.refs_7_), channel_id=1, source_target_pairs={{1,0},{2,1},{3,2},{4,3},{5,4},{6,5},{7,6},{0,7},{9,8},{10,9},{11,1... | collective-permute-start | bytes 442376 | tf_op jit(solution)/shard_map/ppermute | solution.py:286
  13.2 1.5 %collective-permute-start.7 = (bf16[32,2304]{1,0:T(8,128)(2,1)S(1)}, bf16[32,2304]{1,0:T(8,128)(2,1)S(1)}, u32[]{:S(2)}, u32[]{:S(2)}) collective-permute-start(bf16[32,2304]{1,0:T(8,128)(2,1)S(1)} %pad_maximum_fusion.refs_0_), channel_id=1, source_target_pairs={{1,0},{2,1},{3,2},{4,3},{5,4},{6,5},{7,6},{0,7},{9,8},{10,9},{11,1... | collective-permute-start | bytes 442376 | tf_op jit(solution)/shard_map/ppermute | solution.py:286
  15.4 3.5 %collective-permute-start.10 = (bf16[32,2304]{1,0:T(8,128)(2,1)S(1)}, bf16[32,2304]{1,0:T(8,128)(2,1)S(1)}, u32[]{:S(2)}, u32[]{:S(2)}) collective-permute-start(bf16[32,2304]{1,0:T(8,128)(2,1)S(1)} %collective-permute-done.8.refs_9_), channel_id=1, source_target_pairs={{1,0},{2,1},{3,2},{4,3},{5,4},{6,5},{7,6},{0,7},{9,8},{10,9},{11,1... | collective-permute-start | bytes 442376 | tf_op jit(solution)/shard_map/ppermute | solution.py:286
  18.9 3.2 %collective-permute-start.9 = (bf16[32,2304]{1,0:T(8,128)(2,1)S(1)}, bf16[32,2304]{1,0:T(8,128)(2,1)S(1)}, u32[]{:S(2)}, u32[]{:S(2)}) collective-permute-start(bf16[32,2304]{1,0:T(8,128)(2,1)S(1)} %collective-permute-done.7.refs_8_), channel_id=1, source_target_pairs={{1,0},{2,1},{3,2},{4,3},{5,4},{6,5},{7,6},{0,7},{9,8},{10,9},{11,1... | collective-permute-start | bytes 442376 | tf_op jit(solution)/shard_map/ppermute | solution.py:286
  22.6 2.7 %collective-permute-start.12 = (bf16[32,2304]{1,0:T(8,128)(2,1)S(1)}, bf16[32,2304]{1,0:T(8,128)(2,1)S(1)}, u32[]{:S(2)}, u32[]{:S(2)}) collective-permute-start(bf16[32,2304]{1,0:T(8,128)(2,1)S(1)} %collective-permute-done.10.refs_11_), channel_id=1, source_target_pairs={{1,0},{2,1},{3,2},{4,3},{5,4},{6,5},{7,6},{0,7},{9,8},{10,9},{11,1... | collective-permute-start | bytes 442376 | tf_op jit(solution)/shard_map/ppermute | solution.py:286
  25.3 3.2 %collective-permute-start.11 = (bf16[32,2304]{1,0:T(8,128)(2,1)S(1)}, bf16[32,2304]{1,0:T(8,128)(2,1)S(1)}, u32[]{:S(2)}, u32[]{:S(2)}) collective-permute-start(bf16[32,2304]{1,0:T(8,128)(2,1)S(1)} %collective-permute-done.9.refs_10_), channel_id=1, source_target_pairs={{1,0},{2,1},{3,2},{4,3},{5,4},{6,5},{7,6},{0,7},{9,8},{10,9},{11,1... | collective-permute-start | bytes 442376 | tf_op jit(solution)/shard_map/ppermute | solution.py:286
  28.8 3.2 %collective-permute-start.14 = (bf16[32,2304]{1,0:T(8,128)(2,1)S(1)}, bf16[32,2304]{1,0:T(8,128)(2,1)S(1)}, u32[]{:S(2)}, u32[]{:S(2)}) collective-permute-start(bf16[32,2304]{1,0:T(8,128)(2,1)S(1)} %collective-permute-done.12.refs_13_), channel_id=1, source_target_pairs={{1,0},{2,1},{3,2},{4,3},{5,4},{6,5},{7,6},{0,7},{9,8},{10,9},{11,1... | collective-permute-start | bytes 442376 | tf_op jit(solution)/shard_map/ppermute | solution.py:303
  32.1 1.7 %collective-permute-done.6.refs_6_ = bf16[32,2304]{1,0:T(8,128)(2,1)S(1)} collective-permute-done((bf16[32,2304]{1,0:T(8,128)(2,1)S(1)}, bf16[32,2304]{1,0:T(8,128)(2,1)S(1)}, u32[]{:S(2)}, u32[]{:S(2)}) %collective-permute-start.6) | collective-permute-done | bytes 147488 | tf_op jit(solution)/shard_map/ppermute | solution.py:286
  33.7 3.4 %shard_map.74 = (f32[224,2304]{1,0:T(8,128)S(1)}, f32[224,2304]{1,0:T(8,128)S(1)}) custom-call(bf16[32,2304]{1,0:T(8,128)(2,1)S(1)} %pad_maximum_fusion.refs_0_, bf16[32,2304]{1,0:T(8,128)(2,1)S(1)} %collective-permute-done.refs_1_, bf16[32,2304]{1,0:T(8,128)(2,1)S(1)} %collective-permute-done.2.refs_2_, ...), custom_call_target="tpu_custom_call" | custom-call | flops 3112173568 | bytes 100000 | tf_op jit(solution)/shard_map/pallas_call | solution.py:112
  37.1 5.4 %collective-permute-start.16 = (f32[224,2304]{1,0:T(8,128)S(1)}, f32[224,2304]{1,0:T(8,128)S(1)}, u32[]{:S(2)}, u32[]{:S(2)}) collective-permute-start(f32[224,2304]{1,0:T(8,128)S(1)} %get-tuple-element.28), channel_id=1, source_target_pairs={{0,16},{16,0},{32,48},{48,32},{64,80},{80,64},{96,112},{112,96},{1... | collective-permute-start | bytes 6193160 | tf_op jit(solution)/shard_map/ppermute | solution.py:294
  42.6 2.2 %shard_map.75 = (f32[32,2304]{1,0:T(8,128)S(1)}, f32[32,2304]{1,0:T(8,128)S(1)}) custom-call(bf16[32,2304]{1,0:T(8,128)(2,1)S(1)} %collective-permute-done.13.refs_0_, bf16[32,2304]{1,0:T(8,128)(2,1)S(1)} %collective-permute-done.14.refs_1_, bf16[1792,1792]{1,0:T(8,128)(2,1)S(1)} %get-tuple-element.20.refs_14_.refs_2_, ...), custom_call_target="tpu_custom_call" | custom-call | flops 444596224 | bytes 100000 | tf_op jit(solution)/shard_map/pallas_call | solution.py:112
  44.9 1.4 %collective-permute-done.16.got = f32[224,2304]{1,0:T(8,128)S(1)} collective-permute-done((f32[224,2304]{1,0:T(8,128)S(1)}, f32[224,2304]{1,0:T(8,128)S(1)}, u32[]{:S(2)}, u32[]{:S(2)}) %collective-permute-start.16) | collective-permute-done | bytes 2064416 | tf_op jit(solution)/shard_map/ppermute | solution.py:294
  47.1 24.9 %all_to_all.20.codes = s16[8,32,2432]{2,1,0:T(8,128)(2,1)S(1)} all-to-all(s16[8,32,2432]{2,1,0:T(8,128)(2,1)S(1)} %shard_map.77), channel_id=1, replica_groups={{0,32,64,96,128,160,192,224},{16,48,80,112,144,176,208,240},{1,33,65,97..., dimensions={0} | all-to-all | bytes 2490368 | tf_op jit(solution)/shard_map/all_to_all | solution.py:308
  72.5 20.0 %all_to_all.21.own = s16[8,32,2432]{2,1,0:T(8,128)(2,1)S(1)} all-to-all(s16[8,32,2432]{2,1,0:T(8,128)(2,1)S(1)} %shard_map.78), channel_id=1, replica_groups={{0,32,64,96,128,160,192,224},{16,48,80,112,144,176,208,240},{1,33,65,97..., dimensions={0} | all-to-all | bytes 2490368 | tf_op jit(solution)/shard_map/all_to_all | solution.py:310
  92.5 2.9 %collective-permute-start.17 = (s16[8,32,2432]{2,1,0:T(8,128)(2,1)S(1)}, s16[8,32,2432]{2,1,0:T(8,128)(2,1)S(1)}, u32[]{:S(2)}, u32[]{:S(2)}) collective-permute-start(s16[8,32,2432]{2,1,0:T(8,128)(2,1)S(1)} %all_to_all.21.own), channel_id=1, source_target_pairs={{0,16},{16,0},{32,48},{48,32},{64,80},{80,64},{96,112},{112,96},{1... | collective-permute-start | bytes 3735560 | tf_op jit(solution)/shard_map/ppermute | solution.py:311
  95.3 2.6 %collective-permute-done.17.other = s16[8,32,2432]{2,1,0:T(8,128)(2,1)S(1)} collective-permute-done((s16[8,32,2432]{2,1,0:T(8,128)(2,1)S(1)}, s16[8,32,2432]{2,1,0:T(8,128)(2,1)S(1)}, u32[]{:S(2)}, u32[]{:S(2)}) %collective-permute-start.17) | collective-permute-done | bytes 1245216 | tf_op jit(solution)/shard_map/ppermute | solution.py:311
  97.9 1.6 %shard_map.79 = s16[16,32,640]{2,1,0:T(8,128)(2,1)S(1)} custom-call(s16[8,32,2432]{2,1,0:T(8,128)(2,1)S(1)} %all_to_all.21.own, s16[8,32,2432]{2,1,0:T(8,128)(2,1)S(1)} %collective-permute-done.17.other, bf16[256,1792]{1,0:T(8,128)(2,1)S(1)} %copy-done.1, bf16[256,512]{1,0:T(8,128)(2,1)S(1)} %copy-done.3), custom_call_target="tpu_custom_call" | custom-call | tf_op jit(solution)/shard_map/pallas_call | solution.py:225
  99.6 22.6 %all_to_all.22.codes = s16[16,32,640]{2,1,0:T(8,128)(2,1)S(1)} all-to-all(s16[16,32,640]{2,1,0:T(8,128)(2,1)S(1)} %shard_map.79), channel_id=1, replica_groups=mesh['out'=16,'inp'=16] {'inp'}, dimensions={0} | all-to-all | bytes 1310720 | tf_op jit(solution)/shard_map/all_to_all | solution.py:313
  123.1 13.6 %all_to_all.23 = f32[16,8,128]{2,1,0:T(8,128)S(1)} all-to-all(f32[16,8,128]{2,1,0:T(8,128)S(1)} %shard_map.80), channel_id=1, replica_groups=mesh['out'=16,'inp'=16] {'out'}, dimensions={0} | all-to-all | bytes 131072 | tf_op jit(solution)/shard_map/all_to_all | solution.py:315
  (37 shorter events, 5.0 us)
Async XLA Ops:
  0.9 8.3 %collective-permute-start.1 = (bf16[32,2304]{1,0:T(8,128)(2,1)S(1)}, bf16[32,2304]{1,0:T(8,128)(2,1)S(1)}, u32[]{:S(2)}, u32[]{:S(2)}) collective-permute-start(bf16[32,2304]{1,0:T(8,128)(2,1)S(1)} %pad_maximum_fusion.refs_0_), channel_id=1, source_target_pairs={{0,8},{1,9},{2,10},{3,11},{4,12},{5,13},{6,14},{7,15},{8,0},{9,1},... | collective-permute-start | bytes 442376 | tf_op jit(solution)/shard_map/ppermute | solution.py:276
  3.1 11.7 %collective-permute-start = (bf16[32,2304]{1,0:T(8,128)(2,1)S(1)}, bf16[32,2304]{1,0:T(8,128)(2,1)S(1)}, u32[]{:S(2)}, u32[]{:S(2)}) collective-permute-start(bf16[32,2304]{1,0:T(8,128)(2,1)S(1)} %pad_maximum_fusion.refs_0_), channel_id=1, source_target_pairs={{0,1},{1,2},{2,3},{3,4},{4,5},{5,6},{6,7},{7,0},{8,9},{9,10},{10,1... | collective-permute-start | bytes 442376 | tf_op jit(solution)/shard_map/ppermute | solution.py:286
  4.7 2.8 %copy-start = (bf16[1792,1792]{1,0:T(8,128)(2,1)S(1)}, bf16[1792,1792]{1,0:T(8,128)(2,1)}, u32[]{:S(2)}) copy-start(bf16[1792,1792]{1,0:T(8,128)(2,1)} %basis_in.1) | copy-start | bytes 19267588
  7.5 1.0 copy-start.2
  9.2 6.1 %collective-permute-start.8 = (bf16[32,2304]{1,0:T(8,128)(2,1)S(1)}, bf16[32,2304]{1,0:T(8,128)(2,1)S(1)}, u32[]{:S(2)}, u32[]{:S(2)}) collective-permute-start(bf16[32,2304]{1,0:T(8,128)(2,1)S(1)} %collective-permute-done.1.refs_7_), channel_id=1, source_target_pairs={{1,0},{2,1},{3,2},{4,3},{5,4},{6,5},{7,6},{0,7},{9,8},{10,9},{11,1... | collective-permute-start | bytes 442376 | tf_op jit(solution)/shard_map/ppermute | solution.py:286
  13.2 5.6 %collective-permute-start.7 = (bf16[32,2304]{1,0:T(8,128)(2,1)S(1)}, bf16[32,2304]{1,0:T(8,128)(2,1)S(1)}, u32[]{:S(2)}, u32[]{:S(2)}) collective-permute-start(bf16[32,2304]{1,0:T(8,128)(2,1)S(1)} %pad_maximum_fusion.refs_0_), channel_id=1, source_target_pairs={{1,0},{2,1},{3,2},{4,3},{5,4},{6,5},{7,6},{0,7},{9,8},{10,9},{11,1... | collective-permute-start | bytes 442376 | tf_op jit(solution)/shard_map/ppermute | solution.py:286
  14.7 7.3 %collective-permute-start.2 = (bf16[32,2304]{1,0:T(8,128)(2,1)S(1)}, bf16[32,2304]{1,0:T(8,128)(2,1)S(1)}, u32[]{:S(2)}, u32[]{:S(2)}) collective-permute-start(bf16[32,2304]{1,0:T(8,128)(2,1)S(1)} %collective-permute-done.1.refs_7_), channel_id=1, source_target_pairs={{0,1},{1,2},{2,3},{3,4},{4,5},{5,6},{6,7},{7,0},{8,9},{9,10},{10,1... | collective-permute-start | bytes 442376 | tf_op jit(solution)/shard_map/ppermute | solution.py:286
  14.7 7.9 %collective-permute-start.3 = (bf16[32,2304]{1,0:T(8,128)(2,1)S(1)}, bf16[32,2304]{1,0:T(8,128)(2,1)S(1)}, u32[]{:S(2)}, u32[]{:S(2)}) collective-permute-start(bf16[32,2304]{1,0:T(8,128)(2,1)S(1)} %collective-permute-done.refs_1_), channel_id=1, source_target_pairs={{0,1},{1,2},{2,3},{3,4},{4,5},{5,6},{6,7},{7,0},{8,9},{9,10},{10,1... | collective-permute-start | bytes 442376 | tf_op jit(solution)/shard_map/ppermute | solution.py:286
  15.4 7.3 %collective-permute-start.10 = (bf16[32,2304]{1,0:T(8,128)(2,1)S(1)}, bf16[32,2304]{1,0:T(8,128)(2,1)S(1)}, u32[]{:S(2)}, u32[]{:S(2)}) collective-permute-start(bf16[32,2304]{1,0:T(8,128)(2,1)S(1)} %collective-permute-done.8.refs_9_), channel_id=1, source_target_pairs={{1,0},{2,1},{3,2},{4,3},{5,4},{6,5},{7,6},{0,7},{9,8},{10,9},{11,1... | collective-permute-start | bytes 442376 | tf_op jit(solution)/shard_map/ppermute | solution.py:286
  18.9 6.4 %collective-permute-start.9 = (bf16[32,2304]{1,0:T(8,128)(2,1)S(1)}, bf16[32,2304]{1,0:T(8,128)(2,1)S(1)}, u32[]{:S(2)}, u32[]{:S(2)}) collective-permute-start(bf16[32,2304]{1,0:T(8,128)(2,1)S(1)} %collective-permute-done.7.refs_8_), channel_id=1, source_target_pairs={{1,0},{2,1},{3,2},{4,3},{5,4},{6,5},{7,6},{0,7},{9,8},{10,9},{11,1... | collective-permute-start | bytes 442376 | tf_op jit(solution)/shard_map/ppermute | solution.py:286
  22.0 6.5 %collective-permute-start.4 = (bf16[32,2304]{1,0:T(8,128)(2,1)S(1)}, bf16[32,2304]{1,0:T(8,128)(2,1)S(1)}, u32[]{:S(2)}, u32[]{:S(2)}) collective-permute-start(bf16[32,2304]{1,0:T(8,128)(2,1)S(1)} %collective-permute-done.2.refs_2_), channel_id=1, source_target_pairs={{0,1},{1,2},{2,3},{3,4},{4,5},{5,6},{6,7},{7,0},{8,9},{9,10},{10,1... | collective-permute-start | bytes 442376 | tf_op jit(solution)/shard_map/ppermute | solution.py:286
  22.6 6.2 %collective-permute-start.5 = (bf16[32,2304]{1,0:T(8,128)(2,1)S(1)}, bf16[32,2304]{1,0:T(8,128)(2,1)S(1)}, u32[]{:S(2)}, u32[]{:S(2)}) collective-permute-start(bf16[32,2304]{1,0:T(8,128)(2,1)S(1)} %collective-permute-done.3.refs_3_), channel_id=1, source_target_pairs={{0,1},{1,2},{2,3},{3,4},{4,5},{5,6},{6,7},{7,0},{8,9},{9,10},{10,1... | collective-permute-start | bytes 442376 | tf_op jit(solution)/shard_map/ppermute | solution.py:286
  22.6 6.2 %collective-permute-start.12 = (bf16[32,2304]{1,0:T(8,128)(2,1)S(1)}, bf16[32,2304]{1,0:T(8,128)(2,1)S(1)}, u32[]{:S(2)}, u32[]{:S(2)}) collective-permute-start(bf16[32,2304]{1,0:T(8,128)(2,1)S(1)} %collective-permute-done.10.refs_11_), channel_id=1, source_target_pairs={{1,0},{2,1},{3,2},{4,3},{5,4},{6,5},{7,6},{0,7},{9,8},{10,9},{11,1... | collective-permute-start | bytes 442376 | tf_op jit(solution)/shard_map/ppermute | solution.py:286
  25.3 6.8 %collective-permute-start.11 = (bf16[32,2304]{1,0:T(8,128)(2,1)S(1)}, bf16[32,2304]{1,0:T(8,128)(2,1)S(1)}, u32[]{:S(2)}, u32[]{:S(2)}) collective-permute-start(bf16[32,2304]{1,0:T(8,128)(2,1)S(1)} %collective-permute-done.9.refs_10_), channel_id=1, source_target_pairs={{1,0},{2,1},{3,2},{4,3},{5,4},{6,5},{7,6},{0,7},{9,8},{10,9},{11,1... | collective-permute-start | bytes 442376 | tf_op jit(solution)/shard_map/ppermute | solution.py:286
  28.5 5.2 %collective-permute-start.6 = (bf16[32,2304]{1,0:T(8,128)(2,1)S(1)}, bf16[32,2304]{1,0:T(8,128)(2,1)S(1)}, u32[]{:S(2)}, u32[]{:S(2)}) collective-permute-start(bf16[32,2304]{1,0:T(8,128)(2,1)S(1)} %collective-permute-done.4.refs_4_), channel_id=1, source_target_pairs={{0,1},{1,2},{2,3},{3,4},{4,5},{5,6},{6,7},{7,0},{8,9},{9,10},{10,1... | collective-permute-start | bytes 442376 | tf_op jit(solution)/shard_map/ppermute | solution.py:286
  28.8 8.3 %collective-permute-start.13 = (bf16[32,2304]{1,0:T(8,128)(2,1)S(1)}, bf16[32,2304]{1,0:T(8,128)(2,1)S(1)}, u32[]{:S(2)}, u32[]{:S(2)}) collective-permute-start(bf16[32,2304]{1,0:T(8,128)(2,1)S(1)} %collective-permute-done.5.refs_5_), channel_id=1, source_target_pairs={{0,1},{1,2},{2,3},{3,4},{4,5},{5,6},{6,7},{7,0},{8,9},{9,10},{10,1... | collective-permute-start | bytes 442376 | tf_op jit(solution)/shard_map/ppermute | solution.py:302
  28.8 8.3 %collective-permute-start.14 = (bf16[32,2304]{1,0:T(8,128)(2,1)S(1)}, bf16[32,2304]{1,0:T(8,128)(2,1)S(1)}, u32[]{:S(2)}, u32[]{:S(2)}) collective-permute-start(bf16[32,2304]{1,0:T(8,128)(2,1)S(1)} %collective-permute-done.12.refs_13_), channel_id=1, source_target_pairs={{1,0},{2,1},{3,2},{4,3},{5,4},{6,5},{7,6},{0,7},{9,8},{10,9},{11,1... | collective-permute-start | bytes 442376 | tf_op jit(solution)/shard_map/ppermute | solution.py:303
  37.1 9.2 %collective-permute-start.16 = (f32[224,2304]{1,0:T(8,128)S(1)}, f32[224,2304]{1,0:T(8,128)S(1)}, u32[]{:S(2)}, u32[]{:S(2)}) collective-permute-start(f32[224,2304]{1,0:T(8,128)S(1)} %get-tuple-element.28), channel_id=1, source_target_pairs={{0,16},{16,0},{32,48},{48,32},{64,80},{80,64},{96,112},{112,96},{1... | collective-permute-start | bytes 6193160 | tf_op jit(solution)/shard_map/ppermute | solution.py:294
  44.8 2.0 %collective-permute-start.15 = (f32[32,2304]{1,0:T(8,128)S(1)}, f32[32,2304]{1,0:T(8,128)S(1)}, u32[]{:S(2)}, u32[]{:S(2)}) collective-permute-start(f32[32,2304]{1,0:T(8,128)S(1)} %get-tuple-element.26), channel_id=1, source_target_pairs={{0,16},{16,0},{32,48},{48,32},{64,80},{80,64},{96,112},{112,96},{1... | collective-permute-start | bytes 884744 | tf_op jit(solution)/shard_map/ppermute | solution.py:294
  72.4 25.5 %copy-start.1 = (bf16[256,1792]{1,0:T(8,128)(2,1)S(1)}, bf16[256,1792]{1,0:T(8,128)(2,1)}, u32[]{:S(2)}) copy-start(bf16[256,1792]{1,0:T(8,128)(2,1)} %acts.1) | copy-start | bytes 2752516
  72.4 25.5 %copy-start.3 = (bf16[256,512]{1,0:T(8,128)(2,1)S(1)}, bf16[256,512]{1,0:T(8,128)(2,1)}, u32[]{:S(2)}) copy-start(bf16[256,512]{1,0:T(8,128)(2,1)} %grads.1) | copy-start | bytes 786436
  92.5 5.4 %collective-permute-start.17 = (s16[8,32,2432]{2,1,0:T(8,128)(2,1)S(1)}, s16[8,32,2432]{2,1,0:T(8,128)(2,1)S(1)}, u32[]{:S(2)}, u32[]{:S(2)}) collective-permute-start(s16[8,32,2432]{2,1,0:T(8,128)(2,1)S(1)} %all_to_all.21.own), channel_id=1, source_target_pairs={{0,16},{16,0},{32,48},{48,32},{64,80},{80,64},{96,112},{112,96},{1... | collective-permute-start | bytes 3735560 | tf_op jit(solution)/shard_map/ppermute | solution.py:311
  99.6 22.6 %copy-start.4 = (s32[16]{0:T(128)S(1)}, s32[16]{0:T(128)}, u32[]{:S(2)}) copy-start(s32[16]{0:T(128)} %lengths.1) | copy-start | bytes 196

commit v3 on v2

--- a/solution.py
+++ b/solution.py
@@ -75,7 +75,7 @@
         scratch_shapes=[pltpu.SemaphoreType.DMA((2,))],
         compiler_params=params(16),
         cost_estimate=BRIEF,
-    )(basis_in, basis_out)
+    )(*[pltpu.with_memory_space_constraint(x, pltpu.HBM) for x in (basis_in, basis_out)])
 
 
 def rotate_kernel(count, *refs):
@@ -184,12 +184,13 @@
     )(codes)
 
 
-def project_kernel(own, other, acts, grads, out):
-    core = core_id()
+def project_kernel(is_own, *refs):
+    codes, acts, grads, out = refs[0], refs[1], refs[2], refs[-1]
+    half = core_id() if is_own else 1 - core_id()
     place = lax.axis_index("inp")
     x_lo, z = place // 8, lax.rem(place, 8)
     in_width, tokens = acts.shape[1], acts.shape[0]
-    width = own.shape[2] - PAD
+    width = codes.shape[2] - PAD
     contract = (((1,), (1,)), ((), ()))
 
     def side(codes, unit, data):
@@ -201,34 +202,35 @@
         got += lax.dot_general(low, data, contract, preferred_element_type=jnp.float32)
         return got * unit
 
-    for codes, half in ((own, core), (other, 1 - core)):
-        rows = codes.shape[0] * RANK
-        unit_in, unit_out = units(codes[:, :, width:].reshape(rows, PAD))
-        side_in = side(codes[:, :, :in_width].reshape(rows, in_width), unit_in, acts)
-        side_out = side(codes[:, :, in_width:width].reshape(rows, width - in_width), unit_out, grads)
-        level_in, level_out = level_of(side_in), level_of(side_out)
-        code_in, code_out = encode(side_in, level_in), encode(side_out, level_out)
-        tail = pack_levels(level_in, level_out)
-        sign = 2 * half - 1
-        for slot in range(8):
-            away = (slot + 1) // 2
-            cross = (slot + 1) % 2 if 0 < slot < 7 else half
-            target = lax.rem(x_lo + cross, 2) * 8 + lax.rem(z + sign * away + 8, 8)
-            span = slice(slot * RANK, (slot + 1) * RANK)
-            out[target, :, 0:tokens] = code_in[span]
-            out[target, :, tokens : 2 * tokens] = code_out[span]
-            out[target, :, 2 * tokens :] = tail[span]
-
-
-def project(own, other, acts, grads):
+    rows = codes.shape[0] * RANK
+    unit_in, unit_out = units(codes[:, :, width:].reshape(rows, PAD))
+    side_in = side(codes[:, :, :in_width].reshape(rows, in_width), unit_in, acts)
+    side_out = side(codes[:, :, in_width:width].reshape(rows, width - in_width), unit_out, grads)
+    level_in, level_out = level_of(side_in), level_of(side_out)
+    code_in, code_out = encode(side_in, level_in), encode(side_out, level_out)
+    tail = pack_levels(level_in, level_out)
+    sign = 2 * half - 1
+    for slot in range(8):
+        away = (slot + 1) // 2
+        cross = (slot + 1) % 2 if 0 < slot < 7 else half
+        target = lax.rem(x_lo + cross, 2) * 8 + lax.rem(z + sign * away + 8, 8)
+        span = slice(slot * RANK, (slot + 1) * RANK)
+        out[target, :, 0:tokens] = code_in[span]
+        out[target, :, tokens : 2 * tokens] = code_out[span]
+        out[target, :, 2 * tokens :] = tail[span]
+
+
+def project(codes, acts, grads, *filled):
     tokens = acts.shape[0]
     return pl.pallas_call(
-        project_kernel,
-        in_specs=[VMEM] * 4,
+        functools.partial(project_kernel, not filled),
+        in_specs=[VMEM] * (3 + len(filled)),
         out_specs=VMEM,
         out_shape=jax.ShapeDtypeStruct((16, RANK, 2 * tokens + PAD), jnp.int16),
+        input_output_aliases={3: 0} if filled else {},
         compiler_params=params(40),
-    )(own, other, acts, grads)
+        cost_estimate=BRIEF,
+    )(codes, acts, grads, *filled)
 
 
 def score_kernel(lengths, codes, out):
@@ -309,7 +311,7 @@
     codes = resum(codes, in_width)
     own = lax.all_to_all(codes, "out", 0, 0, tiled=True, axis_index_groups=CHIPS)
     sibling = lax.ppermute(own, "out", CORES)
-    sides = project(own, sibling, acts, grads)
+    sides = project(sibling, acts, grads, project(own, acts, grads))
     sides = lax.all_to_all(sides, "inp", 0, 0, tiled=True)
     sums = score(lengths, sides)
     sums = lax.all_to_all(sums, "out", 0, 0, tiled=True)

time: 138 us -> 135 us (0.978)
  local copies, waits for them, and re-layouts: 3.88 us -> 0.02 us
  Pallas kernels: 9.98 us -> 12.7 us
    unnamed x10 -> x6, local copies, waits for them, and re-layouts: 3.88 us -> 0.02 us
    pallas_call x1, Pallas kernels: 0.65 us -> 2.98 us  [stage(): pl.pallas_call(stage_kernel, in_specs=[pl.BlockSpec(memory_space=pltpu.HB...]
    ppermute x12, waiting for transfers between devices: 3.2 us -> 5.22 us  [hop(): return (lax.ppermute(up, 'inp', UP), lax.ppermute(down, 'inp', DOWN))]
  transfers between devices with their start and end apart: 18 -> 18, of which waited for: 6 -> 6; matrix products, arithmetic and copies ran while one was open for 0% -> 0% of each run, Pallas kernels for 5% -> 7%
where the time goes in v3:
time: 135 us
  blocking collectives  80.3 us (59%)
  starting transfers between devices  32.2 us (24%)
  Pallas kernels  12.7 us (9%)
  waiting for transfers between devices  8.2 us (6%)
  other arithmetic  1.48 us (1%)
    all_to_all x2, blocking collectives, per_device(): lax.all_to_all(codes, 'out', 0, 0, tiled=True, axis_index_groups=CHIPS)  45.2 us
    all_to_all x1, blocking collectives, per_device(): sides = lax.all_to_all(sides, 'inp', 0, 0, tiled=True)  21.6 us
    ppermute x12, starting transfers between devices, hop(): return (lax.ppermute(up, 'inp', UP), lax.ppermute(down, 'inp', DOWN))  18.5 us
    all_to_all x1, blocking collectives, per_device(): sums = lax.all_to_all(sums, 'out', 0, 0, tiled=True)  13.5 us
    pallas_call x2, Pallas kernels, rotate(): pl.pallas_call(functools.partial(rotate_kernel, count), in_specs=[VMEM] *...  5.58 us
    ppermute x2, starting transfers between devices, finish(): return code(keep, lax.ppermute(send, 'out', CORES), in_width, *done)  5.38 us
    ppermute x12, waiting for transfers between devices, hop(): return (lax.ppermute(up, 'inp', UP), lax.ppermute(down, 'inp', DOWN))  5.22 us
    ppermute x1, starting transfers between devices, per_device(): b4 = lax.ppermute(b3[1], 'inp', DOWN)  3.29 us
  transfers between devices with their start and end apart: 18, of which 6 were waited for; matrix products, arithmetic and copies ran while one was open for 0% of the time, Pallas kernels for 7%

profile of v3, /device:TPU:1, one launch (start us, length us, event | category | flops | bytes accessed | tf_op | source)
XLA Modules:
  0.0 135.0 jit_solution(13074608905426730615)
XLA Ops:
  0.9 2.1 %collective-permute-start.1 = (bf16[32,2304]{1,0:T(8,128)(2,1)S(1)}, bf16[32,2304]{1,0:T(8,128)(2,1)S(1)}, u32[]{:S(2)}, u32[]{:S(2)}) collective-permute-start(bf16[32,2304]{1,0:T(8,128)(2,1)S(1)} %pad_maximum_fusion.refs_0_), channel_id=1, source_target_pairs={{0,8},{1,9},{2,10},{3,11},{4,12},{5,13},{6,14},{7,15},{8,0},{9,1},... | collective-permute-start | bytes 442376 | tf_op jit(solution)/shard_map/ppermute | solution.py:278
  3.1 1.6 %collective-permute-start = (bf16[32,2304]{1,0:T(8,128)(2,1)S(1)}, bf16[32,2304]{1,0:T(8,128)(2,1)S(1)}, u32[]{:S(2)}, u32[]{:S(2)}) collective-permute-start(bf16[32,2304]{1,0:T(8,128)(2,1)S(1)} %pad_maximum_fusion.refs_0_), channel_id=1, source_target_pairs={{0,1},{1,2},{2,3},{3,4},{4,5},{5,6},{6,7},{7,0},{8,9},{9,10},{10,1... | collective-permute-start | bytes 442376 | tf_op jit(solution)/shard_map/ppermute | solution.py:288
  4.7 3.0 %shard_map.73 = (bf16[1792,1792]{1,0:T(8,128)(2,1)S(1)}, bf16[512,512]{1,0:T(8,128)(2,1)S(1)}) custom-call(bf16[1792,1792]{1,0:T(8,128)(2,1)} %basis_in.1, bf16[512,512]{1,0:T(8,128)(2,1)} %basis_out.1), custom_call_target="tpu_custom_call" | custom-call | flops 100000000 | bytes 100000 | tf_op jit(solution)/shard_map/pallas_call | solution.py:70
  7.7 4.4 %collective-permute-start.8 = (bf16[32,2304]{1,0:T(8,128)(2,1)S(1)}, bf16[32,2304]{1,0:T(8,128)(2,1)S(1)}, u32[]{:S(2)}, u32[]{:S(2)}) collective-permute-start(bf16[32,2304]{1,0:T(8,128)(2,1)S(1)} %collective-permute-done.1.refs_7_), channel_id=1, source_target_pairs={{1,0},{2,1},{3,2},{4,3},{5,4},{6,5},{7,6},{0,7},{9,8},{10,9},{11,1... | collective-permute-start | bytes 442376 | tf_op jit(solution)/shard_map/ppermute | solution.py:288
  12.1 1.0 collective-permute-start.7
  14.2 3.1 %collective-permute-start.10 = (bf16[32,2304]{1,0:T(8,128)(2,1)S(1)}, bf16[32,2304]{1,0:T(8,128)(2,1)S(1)}, u32[]{:S(2)}, u32[]{:S(2)}) collective-permute-start(bf16[32,2304]{1,0:T(8,128)(2,1)S(1)} %collective-permute-done.8.refs_9_), channel_id=1, source_target_pairs={{1,0},{2,1},{3,2},{4,3},{5,4},{6,5},{7,6},{0,7},{9,8},{10,9},{11,1... | collective-permute-start | bytes 442376 | tf_op jit(solution)/shard_map/ppermute | solution.py:288
  17.4 3.0 %collective-permute-start.9 = (bf16[32,2304]{1,0:T(8,128)(2,1)S(1)}, bf16[32,2304]{1,0:T(8,128)(2,1)S(1)}, u32[]{:S(2)}, u32[]{:S(2)}) collective-permute-start(bf16[32,2304]{1,0:T(8,128)(2,1)S(1)} %collective-permute-done.7.refs_8_), channel_id=1, source_target_pairs={{1,0},{2,1},{3,2},{4,3},{5,4},{6,5},{7,6},{0,7},{9,8},{10,9},{11,1... | collective-permute-start | bytes 442376 | tf_op jit(solution)/shard_map/ppermute | solution.py:288
  21.1 2.7 %collective-permute-start.12 = (bf16[32,2304]{1,0:T(8,128)(2,1)S(1)}, bf16[32,2304]{1,0:T(8,128)(2,1)S(1)}, u32[]{:S(2)}, u32[]{:S(2)}) collective-permute-start(bf16[32,2304]{1,0:T(8,128)(2,1)S(1)} %collective-permute-done.10.refs_11_), channel_id=1, source_target_pairs={{1,0},{2,1},{3,2},{4,3},{5,4},{6,5},{7,6},{0,7},{9,8},{10,9},{11,1... | collective-permute-start | bytes 442376 | tf_op jit(solution)/shard_map/ppermute | solution.py:288
  23.8 2.2 %collective-permute-start.11 = (bf16[32,2304]{1,0:T(8,128)(2,1)S(1)}, bf16[32,2304]{1,0:T(8,128)(2,1)S(1)}, u32[]{:S(2)}, u32[]{:S(2)}) collective-permute-start(bf16[32,2304]{1,0:T(8,128)(2,1)S(1)} %collective-permute-done.9.refs_10_), channel_id=1, source_target_pairs={{1,0},{2,1},{3,2},{4,3},{5,4},{6,5},{7,6},{0,7},{9,8},{10,9},{11,1... | collective-permute-start | bytes 442376 | tf_op jit(solution)/shard_map/ppermute | solution.py:288
  26.0 1.1 collective-permute-done.5.refs_5_
  27.1 3.3 %collective-permute-start.14 = (bf16[32,2304]{1,0:T(8,128)(2,1)S(1)}, bf16[32,2304]{1,0:T(8,128)(2,1)S(1)}, u32[]{:S(2)}, u32[]{:S(2)}) collective-permute-start(bf16[32,2304]{1,0:T(8,128)(2,1)S(1)} %collective-permute-done.12.refs_13_), channel_id=1, source_target_pairs={{1,0},{2,1},{3,2},{4,3},{5,4},{6,5},{7,6},{0,7},{9,8},{10,9},{11,1... | collective-permute-start | bytes 442376 | tf_op jit(solution)/shard_map/ppermute | solution.py:305
  30.4 2.7 %collective-permute-done.6.refs_6_ = bf16[32,2304]{1,0:T(8,128)(2,1)S(1)} collective-permute-done((bf16[32,2304]{1,0:T(8,128)(2,1)S(1)}, bf16[32,2304]{1,0:T(8,128)(2,1)S(1)}, u32[]{:S(2)}, u32[]{:S(2)}) %collective-permute-start.6) | collective-permute-done | bytes 147488 | tf_op jit(solution)/shard_map/ppermute | solution.py:288
  33.1 3.4 %shard_map.74 = (f32[224,2304]{1,0:T(8,128)S(1)}, f32[224,2304]{1,0:T(8,128)S(1)}) custom-call(bf16[32,2304]{1,0:T(8,128)(2,1)S(1)} %pad_maximum_fusion.refs_0_, bf16[32,2304]{1,0:T(8,128)(2,1)S(1)} %collective-permute-done.refs_1_, bf16[32,2304]{1,0:T(8,128)(2,1)S(1)} %collective-permute-done.2.refs_2_, ...), custom_call_target="tpu_custom_call" | custom-call | flops 3112173568 | bytes 100000 | tf_op jit(solution)/shard_map/pallas_call | solution.py:112
  36.5 5.3 %collective-permute-start.16 = (f32[224,2304]{1,0:T(8,128)S(1)}, f32[224,2304]{1,0:T(8,128)S(1)}, u32[]{:S(2)}, u32[]{:S(2)}) collective-permute-start(f32[224,2304]{1,0:T(8,128)S(1)} %get-tuple-element.28), channel_id=1, source_target_pairs={{0,16},{16,0},{32,48},{48,32},{64,80},{80,64},{96,112},{112,96},{1... | collective-permute-start | bytes 6193160 | tf_op jit(solution)/shard_map/ppermute | solution.py:296
  41.8 2.2 %shard_map.75 = (f32[32,2304]{1,0:T(8,128)S(1)}, f32[32,2304]{1,0:T(8,128)S(1)}) custom-call(bf16[32,2304]{1,0:T(8,128)(2,1)S(1)} %collective-permute-done.13.refs_0_, bf16[32,2304]{1,0:T(8,128)(2,1)S(1)} %collective-permute-done.14.refs_1_, bf16[1792,1792]{1,0:T(8,128)(2,1)S(1)} %get-tuple-element.20.refs_14_.refs_2_, ...), custom_call_target="tpu_custom_call" | custom-call | flops 444596224 | bytes 100000 | tf_op jit(solution)/shard_map/pallas_call | solution.py:112
  44.1 1.4 %collective-permute-done.16.got = f32[224,2304]{1,0:T(8,128)S(1)} collective-permute-done((f32[224,2304]{1,0:T(8,128)S(1)}, f32[224,2304]{1,0:T(8,128)S(1)}, u32[]{:S(2)}, u32[]{:S(2)}) %collective-permute-start.16) | collective-permute-done | bytes 2064416 | tf_op jit(solution)/shard_map/ppermute | solution.py:296
  46.3 25.2 %all_to_all.20.codes = s16[8,32,2432]{2,1,0:T(8,128)(2,1)S(1)} all-to-all(s16[8,32,2432]{2,1,0:T(8,128)(2,1)S(1)} %shard_map.77), channel_id=1, replica_groups={{0,32,64,96,128,160,192,224},{16,48,80,112,144,176,208,240},{1,33,65,97..., dimensions={0} | all-to-all | bytes 2490368 | tf_op jit(solution)/shard_map/all_to_all | solution.py:310
  72.0 20.0 %all_to_all.21.refs_0_ = s16[8,32,2432]{2,1,0:T(8,128)(2,1)S(1)} all-to-all(s16[8,32,2432]{2,1,0:T(8,128)(2,1)S(1)} %shard_map.78), channel_id=1, replica_groups={{0,32,64,96,128,160,192,224},{16,48,80,112,144,176,208,240},{1,33,65,97..., dimensions={0} | all-to-all | bytes 2490368 | tf_op jit(solution)/shard_map/all_to_all | solution.py:312
  92.0 2.9 %collective-permute-start.17 = (s16[8,32,2432]{2,1,0:T(8,128)(2,1)S(1)}, s16[8,32,2432]{2,1,0:T(8,128)(2,1)S(1)}, u32[]{:S(2)}, u32[]{:S(2)}) collective-permute-start(s16[8,32,2432]{2,1,0:T(8,128)(2,1)S(1)} %all_to_all.21.refs_0_), channel_id=1, source_target_pairs={{0,16},{16,0},{32,48},{48,32},{64,80},{80,64},{96,112},{112,96},{1... | collective-permute-start | bytes 3735560 | tf_op jit(solution)/shard_map/ppermute | solution.py:313
  94.9 1.0 shard_map.79.refs_3_
  95.9 1.6 %collective-permute-done.17.refs_0_ = s16[8,32,2432]{2,1,0:T(8,128)(2,1)S(1)} collective-permute-done((s16[8,32,2432]{2,1,0:T(8,128)(2,1)S(1)}, s16[8,32,2432]{2,1,0:T(8,128)(2,1)S(1)}, u32[]{:S(2)}, u32[]{:S(2)}) %collective-permute-start.17) | collective-permute-done | bytes 1245216 | tf_op jit(solution)/shard_map/ppermute | solution.py:313
  97.4 1.0 shard_map.80
  98.5 21.6 %all_to_all.22.codes = s16[16,32,640]{2,1,0:T(8,128)(2,1)S(1)} all-to-all(s16[16,32,640]{2,1,0:T(8,128)(2,1)S(1)} %shard_map.80), channel_id=1, replica_groups=mesh['out'=16,'inp'=16] {'inp'}, dimensions={0} | all-to-all | bytes 1310720 | tf_op jit(solution)/shard_map/all_to_all | solution.py:315
  120.9 13.5 %all_to_all.23 = f32[16,8,128]{2,1,0:T(8,128)S(1)} all-to-all(f32[16,8,128]{2,1,0:T(8,128)S(1)} %shard_map.81), channel_id=1, replica_groups=mesh['out'=16,'inp'=16] {'out'}, dimensions={0} | all-to-all | bytes 131072 | tf_op jit(solution)/shard_map/all_to_all | solution.py:317
  (34 shorter events, 5.6 us)
Async XLA Ops:
  0.9 6.8 %collective-permute-start.1 = (bf16[32,2304]{1,0:T(8,128)(2,1)S(1)}, bf16[32,2304]{1,0:T(8,128)(2,1)S(1)}, u32[]{:S(2)}, u32[]{:S(2)}) collective-permute-start(bf16[32,2304]{1,0:T(8,128)(2,1)S(1)} %pad_maximum_fusion.refs_0_), channel_id=1, source_target_pairs={{0,8},{1,9},{2,10},{3,11},{4,12},{5,13},{6,14},{7,15},{8,0},{9,1},... | collective-permute-start | bytes 442376 | tf_op jit(solution)/shard_map/ppermute | solution.py:278
  3.1 10.6 %collective-permute-start = (bf16[32,2304]{1,0:T(8,128)(2,1)S(1)}, bf16[32,2304]{1,0:T(8,128)(2,1)S(1)}, u32[]{:S(2)}, u32[]{:S(2)}) collective-permute-start(bf16[32,2304]{1,0:T(8,128)(2,1)S(1)} %pad_maximum_fusion.refs_0_), channel_id=1, source_target_pairs={{0,1},{1,2},{2,3},{3,4},{4,5},{5,6},{6,7},{7,0},{8,9},{9,10},{10,1... | collective-permute-start | bytes 442376 | tf_op jit(solution)/shard_map/ppermute | solution.py:288
  7.7 6.5 %collective-permute-start.8 = (bf16[32,2304]{1,0:T(8,128)(2,1)S(1)}, bf16[32,2304]{1,0:T(8,128)(2,1)S(1)}, u32[]{:S(2)}, u32[]{:S(2)}) collective-permute-start(bf16[32,2304]{1,0:T(8,128)(2,1)S(1)} %collective-permute-done.1.refs_7_), channel_id=1, source_target_pairs={{1,0},{2,1},{3,2},{4,3},{5,4},{6,5},{7,6},{0,7},{9,8},{10,9},{11,1... | collective-permute-start | bytes 442376 | tf_op jit(solution)/shard_map/ppermute | solution.py:288
  12.1 5.2 %collective-permute-start.7 = (bf16[32,2304]{1,0:T(8,128)(2,1)S(1)}, bf16[32,2304]{1,0:T(8,128)(2,1)S(1)}, u32[]{:S(2)}, u32[]{:S(2)}) collective-permute-start(bf16[32,2304]{1,0:T(8,128)(2,1)S(1)} %pad_maximum_fusion.refs_0_), channel_id=1, source_target_pairs={{1,0},{2,1},{3,2},{4,3},{5,4},{6,5},{7,6},{0,7},{9,8},{10,9},{11,1... | collective-permute-start | bytes 442376 | tf_op jit(solution)/shard_map/ppermute | solution.py:288
  13.2 7.1 %collective-permute-start.2 = (bf16[32,2304]{1,0:T(8,128)(2,1)S(1)}, bf16[32,2304]{1,0:T(8,128)(2,1)S(1)}, u32[]{:S(2)}, u32[]{:S(2)}) collective-permute-start(bf16[32,2304]{1,0:T(8,128)(2,1)S(1)} %collective-permute-done.1.refs_7_), channel_id=1, source_target_pairs={{0,1},{1,2},{2,3},{3,4},{4,5},{5,6},{6,7},{7,0},{8,9},{9,10},{10,1... | collective-permute-start | bytes 442376 | tf_op jit(solution)/shard_map/ppermute | solution.py:288
  13.6 7.5 %collective-permute-start.3 = (bf16[32,2304]{1,0:T(8,128)(2,1)S(1)}, bf16[32,2304]{1,0:T(8,128)(2,1)S(1)}, u32[]{:S(2)}, u32[]{:S(2)}) collective-permute-start(bf16[32,2304]{1,0:T(8,128)(2,1)S(1)} %collective-permute-done.refs_1_), channel_id=1, source_target_pairs={{0,1},{1,2},{2,3},{3,4},{4,5},{5,6},{6,7},{7,0},{8,9},{9,10},{10,1... | collective-permute-start | bytes 442376 | tf_op jit(solution)/shard_map/ppermute | solution.py:288
  14.2 6.8 %collective-permute-start.10 = (bf16[32,2304]{1,0:T(8,128)(2,1)S(1)}, bf16[32,2304]{1,0:T(8,128)(2,1)S(1)}, u32[]{:S(2)}, u32[]{:S(2)}) collective-permute-start(bf16[32,2304]{1,0:T(8,128)(2,1)S(1)} %collective-permute-done.8.refs_9_), channel_id=1, source_target_pairs={{1,0},{2,1},{3,2},{4,3},{5,4},{6,5},{7,6},{0,7},{9,8},{10,9},{11,1... | collective-permute-start | bytes 442376 | tf_op jit(solution)/shard_map/ppermute | solution.py:288
  17.4 6.4 %collective-permute-start.9 = (bf16[32,2304]{1,0:T(8,128)(2,1)S(1)}, bf16[32,2304]{1,0:T(8,128)(2,1)S(1)}, u32[]{:S(2)}, u32[]{:S(2)}) collective-permute-start(bf16[32,2304]{1,0:T(8,128)(2,1)S(1)} %collective-permute-done.7.refs_8_), channel_id=1, source_target_pairs={{1,0},{2,1},{3,2},{4,3},{5,4},{6,5},{7,6},{0,7},{9,8},{10,9},{11,1... | collective-permute-start | bytes 442376 | tf_op jit(solution)/shard_map/ppermute | solution.py:288
  20.3 5.7 %collective-permute-start.4 = (bf16[32,2304]{1,0:T(8,128)(2,1)S(1)}, bf16[32,2304]{1,0:T(8,128)(2,1)S(1)}, u32[]{:S(2)}, u32[]{:S(2)}) collective-permute-start(bf16[32,2304]{1,0:T(8,128)(2,1)S(1)} %collective-permute-done.2.refs_2_), channel_id=1, source_target_pairs={{0,1},{1,2},{2,3},{3,4},{4,5},{5,6},{6,7},{7,0},{8,9},{9,10},{10,1... | collective-permute-start | bytes 442376 | tf_op jit(solution)/shard_map/ppermute | solution.py:288
  21.1 6.0 %collective-permute-start.5 = (bf16[32,2304]{1,0:T(8,128)(2,1)S(1)}, bf16[32,2304]{1,0:T(8,128)(2,1)S(1)}, u32[]{:S(2)}, u32[]{:S(2)}) collective-permute-start(bf16[32,2304]{1,0:T(8,128)(2,1)S(1)} %collective-permute-done.3.refs_3_), channel_id=1, source_target_pairs={{0,1},{1,2},{2,3},{3,4},{4,5},{5,6},{6,7},{7,0},{8,9},{9,10},{10,1... | collective-permute-start | bytes 442376 | tf_op jit(solution)/shard_map/ppermute | solution.py:288
  21.1 6.0 %collective-permute-start.12 = (bf16[32,2304]{1,0:T(8,128)(2,1)S(1)}, bf16[32,2304]{1,0:T(8,128)(2,1)S(1)}, u32[]{:S(2)}, u32[]{:S(2)}) collective-permute-start(bf16[32,2304]{1,0:T(8,128)(2,1)S(1)} %collective-permute-done.10.refs_11_), channel_id=1, source_target_pairs={{1,0},{2,1},{3,2},{4,3},{5,4},{6,5},{7,6},{0,7},{9,8},{10,9},{11,1... | collective-permute-start | bytes 442376 | tf_op jit(solution)/shard_map/ppermute | solution.py:288
  23.8 6.6 %collective-permute-start.11 = (bf16[32,2304]{1,0:T(8,128)(2,1)S(1)}, bf16[32,2304]{1,0:T(8,128)(2,1)S(1)}, u32[]{:S(2)}, u32[]{:S(2)}) collective-permute-start(bf16[32,2304]{1,0:T(8,128)(2,1)S(1)} %collective-permute-done.9.refs_10_), channel_id=1, source_target_pairs={{1,0},{2,1},{3,2},{4,3},{5,4},{6,5},{7,6},{0,7},{9,8},{10,9},{11,1... | collective-permute-start | bytes 442376 | tf_op jit(solution)/shard_map/ppermute | solution.py:288
  26.0 7.1 %collective-permute-start.6 = (bf16[32,2304]{1,0:T(8,128)(2,1)S(1)}, bf16[32,2304]{1,0:T(8,128)(2,1)S(1)}, u32[]{:S(2)}, u32[]{:S(2)}) collective-permute-start(bf16[32,2304]{1,0:T(8,128)(2,1)S(1)} %collective-permute-done.4.refs_4_), channel_id=1, source_target_pairs={{0,1},{1,2},{2,3},{3,4},{4,5},{5,6},{6,7},{7,0},{8,9},{9,10},{10,1... | collective-permute-start | bytes 442376 | tf_op jit(solution)/shard_map/ppermute | solution.py:288
  27.1 9.4 %collective-permute-start.13 = (bf16[32,2304]{1,0:T(8,128)(2,1)S(1)}, bf16[32,2304]{1,0:T(8,128)(2,1)S(1)}, u32[]{:S(2)}, u32[]{:S(2)}) collective-permute-start(bf16[32,2304]{1,0:T(8,128)(2,1)S(1)} %collective-permute-done.5.refs_5_), channel_id=1, source_target_pairs={{0,1},{1,2},{2,3},{3,4},{4,5},{5,6},{6,7},{7,0},{8,9},{9,10},{10,1... | collective-permute-start | bytes 442376 | tf_op jit(solution)/shard_map/ppermute | solution.py:304
  27.1 9.4 %collective-permute-start.14 = (bf16[32,2304]{1,0:T(8,128)(2,1)S(1)}, bf16[32,2304]{1,0:T(8,128)(2,1)S(1)}, u32[]{:S(2)}, u32[]{:S(2)}) collective-permute-start(bf16[32,2304]{1,0:T(8,128)(2,1)S(1)} %collective-permute-done.12.refs_13_), channel_id=1, source_target_pairs={{1,0},{2,1},{3,2},{4,3},{5,4},{6,5},{7,6},{0,7},{9,8},{10,9},{11,1... | collective-permute-start | bytes 442376 | tf_op jit(solution)/shard_map/ppermute | solution.py:305
  36.5 9.0 %collective-permute-start.16 = (f32[224,2304]{1,0:T(8,128)S(1)}, f32[224,2304]{1,0:T(8,128)S(1)}, u32[]{:S(2)}, u32[]{:S(2)}) collective-permute-start(f32[224,2304]{1,0:T(8,128)S(1)} %get-tuple-element.28), channel_id=1, source_target_pairs={{0,16},{16,0},{32,48},{48,32},{64,80},{80,64},{96,112},{112,96},{1... | collective-permute-start | bytes 6193160 | tf_op jit(solution)/shard_map/ppermute | solution.py:296
  44.0 2.0 %collective-permute-start.15 = (f32[32,2304]{1,0:T(8,128)S(1)}, f32[32,2304]{1,0:T(8,128)S(1)}, u32[]{:S(2)}, u32[]{:S(2)}) collective-permute-start(f32[32,2304]{1,0:T(8,128)S(1)} %get-tuple-element.26), channel_id=1, source_target_pairs={{0,16},{16,0},{32,48},{48,32},{64,80},{80,64},{96,112},{112,96},{1... | collective-permute-start | bytes 884744 | tf_op jit(solution)/shard_map/ppermute | solution.py:296
  72.0 22.9 %copy-start = (bf16[256,1792]{1,0:T(8,128)(2,1)S(1)}, bf16[256,1792]{1,0:T(8,128)(2,1)}, u32[]{:S(2)}) copy-start(bf16[256,1792]{1,0:T(8,128)(2,1)} %refs_1_.3) | copy-start | bytes 2752516
  72.0 22.9 %copy-start.1 = (bf16[256,512]{1,0:T(8,128)(2,1)S(1)}, bf16[256,512]{1,0:T(8,128)(2,1)}, u32[]{:S(2)}) copy-start(bf16[256,512]{1,0:T(8,128)(2,1)} %refs_2_.3) | copy-start | bytes 786436
  92.0 5.4 %collective-permute-start.17 = (s16[8,32,2432]{2,1,0:T(8,128)(2,1)S(1)}, s16[8,32,2432]{2,1,0:T(8,128)(2,1)S(1)}, u32[]{:S(2)}, u32[]{:S(2)}) collective-permute-start(s16[8,32,2432]{2,1,0:T(8,128)(2,1)S(1)} %all_to_all.21.refs_0_), channel_id=1, source_target_pairs={{0,16},{16,0},{32,48},{48,32},{64,80},{80,64},{96,112},{112,96},{1... | collective-permute-start | bytes 3735560 | tf_op jit(solution)/shard_map/ppermute | solution.py:313
  98.4 21.6 %copy-start.2 = (s32[16]{0:T(128)S(1)}, s32[16]{0:T(128)}, u32[]{:S(2)}) copy-start(s32[16]{0:T(128)} %lengths.1) | copy-start | bytes 196

commit v4 on v3

--- a/solution.py
+++ b/solution.py
@@ -276,28 +276,28 @@
     in_width = basis_in.shape[0]
     mine = jnp.concatenate([query_in.T, query_out.T], axis=1)
     other = lax.ppermute(mine, "inp", ACROSS)
-    other, basis_in, basis_out = lax.optimization_barrier(
-        (other, *stage(basis_in, basis_out))
+
+
+    def hop(ends):
+        up, down = ends
+        return lax.ppermute(up, "inp", UP), lax.ppermute(down, "inp", DOWN)
+
+    def rotated(*ends):
+        firsts, seconds = zip(*ends)
+        return rotate(firsts, seconds, basis_in, basis_out)
+
+    def finish(rotated, *done):
+        keep, send = rotated
+        return code(keep, lax.ppermute(send, "out", CORES), in_width, *done)
+
+    a1 = hop((mine, mine))
+    b1 = hop((other, other))
+    a2 = hop(a1)
+    a2, basis_in, basis_out = lax.optimization_barrier(
+        (a2, *stage(basis_in, basis_out))
     )
     basis_in = pltpu.with_memory_space_constraint(basis_in, pltpu.VMEM)
     basis_out = pltpu.with_memory_space_constraint(basis_out, pltpu.VMEM)
-
-
-    def hop(ends):
-        up, down = ends
-        return lax.ppermute(up, "inp", UP), lax.ppermute(down, "inp", DOWN)
-
-    def rotated(*ends):
-        firsts, seconds = zip(*ends)
-        return rotate(firsts, seconds, basis_in, basis_out)
-
-    def finish(rotated, *done):
-        keep, send = rotated
-        return code(keep, lax.ppermute(send, "out", CORES), in_width, *done)
-
-    a1 = hop((mine, mine))
-    b1 = hop((other, other))
-    a2 = hop(a1)
     b2 = hop(b1)
     a3 = hop(a2)
     b3 = hop(b2)

time: 135 us -> 132 us (0.978)
  waiting for transfers between devices: 8.2 us -> 6.04 us
    ppermute x12, waiting for transfers between devices: 5.22 us -> 3.06 us  [hop(): return (lax.ppermute(up, 'inp', UP), lax.ppermute(down, 'inp', DOWN))]
  transfers between devices with their start and end apart: 18 -> 18, of which waited for: 6 -> 7; matrix products, arithmetic and copies ran while one was open for 0% -> 0% of each run, Pallas kernels for 7% -> 8%
where the time goes in v4:
time: 132 us
  blocking collectives  79.9 us (61%)
  starting transfers between devices  31.9 us (24%)
  Pallas kernels  12.7 us (10%)
  waiting for transfers between devices  6.04 us (5%)
  other arithmetic  1.48 us (1%)
    all_to_all x2, blocking collectives, per_device(): lax.all_to_all(codes, 'out', 0, 0, tiled=True, axis_index_groups=CHIPS)  45.2 us
    all_to_all x1, blocking collectives, per_device(): sides = lax.all_to_all(sides, 'inp', 0, 0, tiled=True)  21.2 us
    ppermute x12, starting transfers between devices, hop(): return (lax.ppermute(up, 'inp', UP), lax.ppermute(down, 'inp', DOWN))  19.2 us
    all_to_all x1, blocking collectives, per_device(): sums = lax.all_to_all(sums, 'out', 0, 0, tiled=True)  13.5 us
    pallas_call x2, Pallas kernels, rotate(): pl.pallas_call(functools.partial(rotate_kernel, count), in_specs=[VMEM] *...  5.58 us
    ppermute x2, starting transfers between devices, finish(): return code(keep, lax.ppermute(send, 'out', CORES), in_width, *done)  4.59 us
    ppermute x1, starting transfers between devices, per_device(): b4 = lax.ppermute(b3[1], 'inp', DOWN)  3.1 us
    ppermute x12, waiting for transfers between devices, hop(): return (lax.ppermute(up, 'inp', UP), lax.ppermute(down, 'inp', DOWN))  3.06 us
  transfers between devices with their start and end apart: 18, of which 7 were waited for; matrix products, arithmetic and copies ran while one was open for 0% of the time, Pallas kernels for 8%

profile of v4, /device:TPU:1, one launch (start us, length us, event | category | flops | bytes accessed | tf_op | source)
XLA Modules:
  0.0 132.2 jit_solution(2562707921950401141)
XLA Ops:
  0.0 0.9 pad_maximum_fusion.refs_0_
  0.9 2.1 %collective-permute-start.1 = (bf16[32,2304]{1,0:T(8,128)(2,1)S(1)}, bf16[32,2304]{1,0:T(8,128)(2,1)S(1)}, u32[]{:S(2)}, u32[]{:S(2)}) collective-permute-start(bf16[32,2304]{1,0:T(8,128)(2,1)S(1)} %pad_maximum_fusion.refs_0_), channel_id=1, source_target_pairs={{0,8},{1,9},{2,10},{3,11},{4,12},{5,13},{6,14},{7,15},{8,0},{9,1},... | collective-permute-start | bytes 442376 | tf_op jit(solution)/shard_map/ppermute | solution.py:278
  3.1 1.6 %collective-permute-start = (bf16[32,2304]{1,0:T(8,128)(2,1)S(1)}, bf16[32,2304]{1,0:T(8,128)(2,1)S(1)}, u32[]{:S(2)}, u32[]{:S(2)}) collective-permute-start(bf16[32,2304]{1,0:T(8,128)(2,1)S(1)} %pad_maximum_fusion.refs_0_), channel_id=1, source_target_pairs={{0,1},{1,2},{2,3},{3,4},{4,5},{5,6},{6,7},{7,0},{8,9},{9,10},{10,1... | collective-permute-start | bytes 442376 | tf_op jit(solution)/shard_map/ppermute | solution.py:283
  4.7 3.9 %collective-permute-start.4 = (bf16[32,2304]{1,0:T(8,128)(2,1)S(1)}, bf16[32,2304]{1,0:T(8,128)(2,1)S(1)}, u32[]{:S(2)}, u32[]{:S(2)}) collective-permute-start(bf16[32,2304]{1,0:T(8,128)(2,1)S(1)} %pad_maximum_fusion.refs_0_), channel_id=1, source_target_pairs={{1,0},{2,1},{3,2},{4,3},{5,4},{6,5},{7,6},{0,7},{9,8},{10,9},{11,1... | collective-permute-start | bytes 442376 | tf_op jit(solution)/shard_map/ppermute | solution.py:283
  8.6 3.5 %collective-permute-start.9 = (bf16[32,2304]{1,0:T(8,128)(2,1)S(1)}, bf16[32,2304]{1,0:T(8,128)(2,1)S(1)}, u32[]{:S(2)}, u32[]{:S(2)}) collective-permute-start(bf16[32,2304]{1,0:T(8,128)(2,1)S(1)} %collective-permute-done.1.refs_7_), channel_id=1, source_target_pairs={{1,0},{2,1},{3,2},{4,3},{5,4},{6,5},{7,6},{0,7},{9,8},{10,9},{11,1... | collective-permute-start | bytes 442376 | tf_op jit(solution)/shard_map/ppermute | solution.py:283
  12.2 2.7 %collective-permute-start.5 = (bf16[32,2304]{1,0:T(8,128)(2,1)S(1)}, bf16[32,2304]{1,0:T(8,128)(2,1)S(1)}, u32[]{:S(2)}, u32[]{:S(2)}) collective-permute-start(bf16[32,2304]{1,0:T(8,128)(2,1)S(1)} %collective-permute-done.4.refs_8_), channel_id=1, source_target_pairs={{1,0},{2,1},{3,2},{4,3},{5,4},{6,5},{7,6},{0,7},{9,8},{10,9},{11,1... | collective-permute-start | bytes 442376 | tf_op jit(solution)/shard_map/ppermute | solution.py:283
  14.9 2.4 %collective-permute-start.10 = (bf16[32,2304]{1,0:T(8,128)(2,1)S(1)}, bf16[32,2304]{1,0:T(8,128)(2,1)S(1)}, u32[]{:S(2)}, u32[]{:S(2)}) collective-permute-start(bf16[32,2304]{1,0:T(8,128)(2,1)S(1)} %collective-permute-done.9.refs_9_), channel_id=1, source_target_pairs={{1,0},{2,1},{3,2},{4,3},{5,4},{6,5},{7,6},{0,7},{9,8},{10,9},{11,1... | collective-permute-start | bytes 442376 | tf_op jit(solution)/shard_map/ppermute | solution.py:283
  17.4 3.0 %shard_map.73 = (bf16[1792,1792]{1,0:T(8,128)(2,1)S(1)}, bf16[512,512]{1,0:T(8,128)(2,1)S(1)}) custom-call(bf16[1792,1792]{1,0:T(8,128)(2,1)} %basis_in.1, bf16[512,512]{1,0:T(8,128)(2,1)} %basis_out.1), custom_call_target="tpu_custom_call" | custom-call | flops 100000000 | bytes 100000 | tf_op jit(solution)/shard_map/pallas_call | solution.py:70
  20.9 3.4 %collective-permute-start.12 = (bf16[32,2304]{1,0:T(8,128)(2,1)S(1)}, bf16[32,2304]{1,0:T(8,128)(2,1)S(1)}, u32[]{:S(2)}, u32[]{:S(2)}) collective-permute-start(bf16[32,2304]{1,0:T(8,128)(2,1)S(1)} %collective-permute-done.10.refs_11_), channel_id=1, source_target_pairs={{1,0},{2,1},{3,2},{4,3},{5,4},{6,5},{7,6},{0,7},{9,8},{10,9},{11,1... | collective-permute-start | bytes 442376 | tf_op jit(solution)/shard_map/ppermute | solution.py:283
  24.6 1.2 collective-permute-start.8
  26.4 3.1 %collective-permute-start.14 = (bf16[32,2304]{1,0:T(8,128)(2,1)S(1)}, bf16[32,2304]{1,0:T(8,128)(2,1)S(1)}, u32[]{:S(2)}, u32[]{:S(2)}) collective-permute-start(bf16[32,2304]{1,0:T(8,128)(2,1)S(1)} %collective-permute-done.12.refs_13_), channel_id=1, source_target_pairs={{1,0},{2,1},{3,2},{4,3},{5,4},{6,5},{7,6},{0,7},{9,8},{10,9},{11,1... | collective-permute-start | bytes 442376 | tf_op jit(solution)/shard_map/ppermute | solution.py:305
  29.7 1.8 %collective-permute-done.8.refs_6_ = bf16[32,2304]{1,0:T(8,128)(2,1)S(1)} collective-permute-done((bf16[32,2304]{1,0:T(8,128)(2,1)S(1)}, bf16[32,2304]{1,0:T(8,128)(2,1)S(1)}, u32[]{:S(2)}, u32[]{:S(2)}) %collective-permute-start.8) | collective-permute-done | bytes 147488 | tf_op jit(solution)/shard_map/ppermute | solution.py:283
  31.5 3.4 %shard_map.74 = (f32[224,2304]{1,0:T(8,128)S(1)}, f32[224,2304]{1,0:T(8,128)S(1)}) custom-call(bf16[32,2304]{1,0:T(8,128)(2,1)S(1)} %pad_maximum_fusion.refs_0_, bf16[32,2304]{1,0:T(8,128)(2,1)S(1)} %collective-permute-done.refs_1_, bf16[32,2304]{1,0:T(8,128)(2,1)S(1)} %collective-permute-done.2.refs_2_, ...), custom_call_target="tpu_custom_call" | custom-call | flops 3112173568 | bytes 100000 | tf_op jit(solution)/shard_map/pallas_call | solution.py:112
  34.9 4.5 %collective-permute-start.16 = (f32[224,2304]{1,0:T(8,128)S(1)}, f32[224,2304]{1,0:T(8,128)S(1)}, u32[]{:S(2)}, u32[]{:S(2)}) collective-permute-start(f32[224,2304]{1,0:T(8,128)S(1)} %get-tuple-element.30), channel_id=1, source_target_pairs={{0,16},{16,0},{32,48},{48,32},{64,80},{80,64},{96,112},{112,96},{1... | collective-permute-start | bytes 6193160 | tf_op jit(solution)/shard_map/ppermute | solution.py:291
  39.4 2.2 %shard_map.75 = (f32[32,2304]{1,0:T(8,128)S(1)}, f32[32,2304]{1,0:T(8,128)S(1)}) custom-call(bf16[32,2304]{1,0:T(8,128)(2,1)S(1)} %collective-permute-done.13.refs_0_, bf16[32,2304]{1,0:T(8,128)(2,1)S(1)} %collective-permute-done.14.refs_1_, bf16[1792,1792]{1,0:T(8,128)(2,1)S(1)} %get-tuple-element.22.refs_14_.refs_2_, ...), custom_call_target="tpu_custom_call" | custom-call | flops 444596224 | bytes 100000 | tf_op jit(solution)/shard_map/pallas_call | solution.py:112
  41.7 1.4 %collective-permute-done.16.got = f32[224,2304]{1,0:T(8,128)S(1)} collective-permute-done((f32[224,2304]{1,0:T(8,128)S(1)}, f32[224,2304]{1,0:T(8,128)S(1)}, u32[]{:S(2)}, u32[]{:S(2)}) %collective-permute-start.16) | collective-permute-done | bytes 2064416 | tf_op jit(solution)/shard_map/ppermute | solution.py:291
  43.9 25.2 %all_to_all.20.codes = s16[8,32,2432]{2,1,0:T(8,128)(2,1)S(1)} all-to-all(s16[8,32,2432]{2,1,0:T(8,128)(2,1)S(1)} %shard_map.77), channel_id=1, replica_groups={{0,32,64,96,128,160,192,224},{16,48,80,112,144,176,208,240},{1,33,65,97..., dimensions={0} | all-to-all | bytes 2490368 | tf_op jit(solution)/shard_map/all_to_all | solution.py:310
  69.6 20.0 %all_to_all.21.refs_0_ = s16[8,32,2432]{2,1,0:T(8,128)(2,1)S(1)} all-to-all(s16[8,32,2432]{2,1,0:T(8,128)(2,1)S(1)} %shard_map.78), channel_id=1, replica_groups={{0,32,64,96,128,160,192,224},{16,48,80,112,144,176,208,240},{1,33,65,97..., dimensions={0} | all-to-all | bytes 2490368 | tf_op jit(solution)/shard_map/all_to_all | solution.py:312
  89.6 2.9 %collective-permute-start.17 = (s16[8,32,2432]{2,1,0:T(8,128)(2,1)S(1)}, s16[8,32,2432]{2,1,0:T(8,128)(2,1)S(1)}, u32[]{:S(2)}, u32[]{:S(2)}) collective-permute-start(s16[8,32,2432]{2,1,0:T(8,128)(2,1)S(1)} %all_to_all.21.refs_0_), channel_id=1, source_target_pairs={{0,16},{16,0},{32,48},{48,32},{64,80},{80,64},{96,112},{112,96},{1... | collective-permute-start | bytes 3735560 | tf_op jit(solution)/shard_map/ppermute | solution.py:313
  92.4 1.0 shard_map.79.refs_3_
  93.4 1.6 %collective-permute-done.17.refs_0_ = s16[8,32,2432]{2,1,0:T(8,128)(2,1)S(1)} collective-permute-done((s16[8,32,2432]{2,1,0:T(8,128)(2,1)S(1)}, s16[8,32,2432]{2,1,0:T(8,128)(2,1)S(1)}, u32[]{:S(2)}, u32[]{:S(2)}) %collective-permute-start.17) | collective-permute-done | bytes 1245216 | tf_op jit(solution)/shard_map/ppermute | solution.py:313
  95.0 1.0 shard_map.80
  96.0 21.2 %all_to_all.22.codes = s16[16,32,640]{2,1,0:T(8,128)(2,1)S(1)} all-to-all(s16[16,32,640]{2,1,0:T(8,128)(2,1)S(1)} %shard_map.80), channel_id=1, replica_groups=mesh['out'=16,'inp'=16] {'inp'}, dimensions={0} | all-to-all | bytes 1310720 | tf_op jit(solution)/shard_map/all_to_all | solution.py:315
  118.1 13.5 %all_to_all.23 = f32[16,8,128]{2,1,0:T(8,128)S(1)} all-to-all(f32[16,8,128]{2,1,0:T(8,128)S(1)} %shard_map.81), channel_id=1, replica_groups=mesh['out'=16,'inp'=16] {'out'}, dimensions={0} | all-to-all | bytes 131072 | tf_op jit(solution)/shard_map/all_to_all | solution.py:317
  (34 shorter events, 4.4 us)
Async XLA Ops:
  0.9 7.7 %collective-permute-start.1 = (bf16[32,2304]{1,0:T(8,128)(2,1)S(1)}, bf16[32,2304]{1,0:T(8,128)(2,1)S(1)}, u32[]{:S(2)}, u32[]{:S(2)}) collective-permute-start(bf16[32,2304]{1,0:T(8,128)(2,1)S(1)} %pad_maximum_fusion.refs_0_), channel_id=1, source_target_pairs={{0,8},{1,9},{2,10},{3,11},{4,12},{5,13},{6,14},{7,15},{8,0},{9,1},... | collective-permute-start | bytes 442376 | tf_op jit(solution)/shard_map/ppermute | solution.py:278
  3.1 9.1 %collective-permute-start = (bf16[32,2304]{1,0:T(8,128)(2,1)S(1)}, bf16[32,2304]{1,0:T(8,128)(2,1)S(1)}, u32[]{:S(2)}, u32[]{:S(2)}) collective-permute-start(bf16[32,2304]{1,0:T(8,128)(2,1)S(1)} %pad_maximum_fusion.refs_0_), channel_id=1, source_target_pairs={{0,1},{1,2},{2,3},{3,4},{4,5},{5,6},{6,7},{7,0},{8,9},{9,10},{10,1... | collective-permute-start | bytes 442376 | tf_op jit(solution)/shard_map/ppermute | solution.py:283
  4.7 7.5 %collective-permute-start.4 = (bf16[32,2304]{1,0:T(8,128)(2,1)S(1)}, bf16[32,2304]{1,0:T(8,128)(2,1)S(1)}, u32[]{:S(2)}, u32[]{:S(2)}) collective-permute-start(bf16[32,2304]{1,0:T(8,128)(2,1)S(1)} %pad_maximum_fusion.refs_0_), channel_id=1, source_target_pairs={{1,0},{2,1},{3,2},{4,3},{5,4},{6,5},{7,6},{0,7},{9,8},{10,9},{11,1... | collective-permute-start | bytes 442376 | tf_op jit(solution)/shard_map/ppermute | solution.py:283
  8.6 6.3 %collective-permute-start.9 = (bf16[32,2304]{1,0:T(8,128)(2,1)S(1)}, bf16[32,2304]{1,0:T(8,128)(2,1)S(1)}, u32[]{:S(2)}, u32[]{:S(2)}) collective-permute-start(bf16[32,2304]{1,0:T(8,128)(2,1)S(1)} %collective-permute-done.1.refs_7_), channel_id=1, source_target_pairs={{1,0},{2,1},{3,2},{4,3},{5,4},{6,5},{7,6},{0,7},{9,8},{10,9},{11,1... | collective-permute-start | bytes 442376 | tf_op jit(solution)/shard_map/ppermute | solution.py:283
  12.1 5.2 %collective-permute-start.2 = (bf16[32,2304]{1,0:T(8,128)(2,1)S(1)}, bf16[32,2304]{1,0:T(8,128)(2,1)S(1)}, u32[]{:S(2)}, u32[]{:S(2)}) collective-permute-start(bf16[32,2304]{1,0:T(8,128)(2,1)S(1)} %collective-permute-done.1.refs_7_), channel_id=1, source_target_pairs={{0,1},{1,2},{2,3},{3,4},{4,5},{5,6},{6,7},{7,0},{8,9},{9,10},{10,1... | collective-permute-start | bytes 442376 | tf_op jit(solution)/shard_map/ppermute | solution.py:283
  12.1 8.2 %collective-permute-start.3 = (bf16[32,2304]{1,0:T(8,128)(2,1)S(1)}, bf16[32,2304]{1,0:T(8,128)(2,1)S(1)}, u32[]{:S(2)}, u32[]{:S(2)}) collective-permute-start(bf16[32,2304]{1,0:T(8,128)(2,1)S(1)} %collective-permute-done.refs_1_), channel_id=1, source_target_pairs={{0,1},{1,2},{2,3},{3,4},{4,5},{5,6},{6,7},{7,0},{8,9},{9,10},{10,1... | collective-permute-start | bytes 442376 | tf_op jit(solution)/shard_map/ppermute | solution.py:283
  12.2 8.2 %collective-permute-start.5 = (bf16[32,2304]{1,0:T(8,128)(2,1)S(1)}, bf16[32,2304]{1,0:T(8,128)(2,1)S(1)}, u32[]{:S(2)}, u32[]{:S(2)}) collective-permute-start(bf16[32,2304]{1,0:T(8,128)(2,1)S(1)} %collective-permute-done.4.refs_8_), channel_id=1, source_target_pairs={{1,0},{2,1},{3,2},{4,3},{5,4},{6,5},{7,6},{0,7},{9,8},{10,9},{11,1... | collective-permute-start | bytes 442376 | tf_op jit(solution)/shard_map/ppermute | solution.py:283
  14.9 6.0 %collective-permute-start.10 = (bf16[32,2304]{1,0:T(8,128)(2,1)S(1)}, bf16[32,2304]{1,0:T(8,128)(2,1)S(1)}, u32[]{:S(2)}, u32[]{:S(2)}) collective-permute-start(bf16[32,2304]{1,0:T(8,128)(2,1)S(1)} %collective-permute-done.9.refs_9_), channel_id=1, source_target_pairs={{1,0},{2,1},{3,2},{4,3},{5,4},{6,5},{7,6},{0,7},{9,8},{10,9},{11,1... | collective-permute-start | bytes 442376 | tf_op jit(solution)/shard_map/ppermute | solution.py:283
  17.4 7.2 %collective-permute-start.6 = (bf16[32,2304]{1,0:T(8,128)(2,1)S(1)}, bf16[32,2304]{1,0:T(8,128)(2,1)S(1)}, u32[]{:S(2)}, u32[]{:S(2)}) collective-permute-start(bf16[32,2304]{1,0:T(8,128)(2,1)S(1)} %collective-permute-done.2.refs_2_), channel_id=1, source_target_pairs={{0,1},{1,2},{2,3},{3,4},{4,5},{5,6},{6,7},{7,0},{8,9},{9,10},{10,1... | collective-permute-start | bytes 442376 | tf_op jit(solution)/shard_map/ppermute | solution.py:283
  20.4 5.9 %collective-permute-start.7 = (bf16[32,2304]{1,0:T(8,128)(2,1)S(1)}, bf16[32,2304]{1,0:T(8,128)(2,1)S(1)}, u32[]{:S(2)}, u32[]{:S(2)}) collective-permute-start(bf16[32,2304]{1,0:T(8,128)(2,1)S(1)} %collective-permute-done.3.refs_3_), channel_id=1, source_target_pairs={{0,1},{1,2},{2,3},{3,4},{4,5},{5,6},{6,7},{7,0},{8,9},{9,10},{10,1... | collective-permute-start | bytes 442376 | tf_op jit(solution)/shard_map/ppermute | solution.py:283
  20.9 5.5 %collective-permute-start.12 = (bf16[32,2304]{1,0:T(8,128)(2,1)S(1)}, bf16[32,2304]{1,0:T(8,128)(2,1)S(1)}, u32[]{:S(2)}, u32[]{:S(2)}) collective-permute-start(bf16[32,2304]{1,0:T(8,128)(2,1)S(1)} %collective-permute-done.10.refs_11_), channel_id=1, source_target_pairs={{1,0},{2,1},{3,2},{4,3},{5,4},{6,5},{7,6},{0,7},{9,8},{10,9},{11,1... | collective-permute-start | bytes 442376 | tf_op jit(solution)/shard_map/ppermute | solution.py:283
  24.3 5.4 %collective-permute-start.11 = (bf16[32,2304]{1,0:T(8,128)(2,1)S(1)}, bf16[32,2304]{1,0:T(8,128)(2,1)S(1)}, u32[]{:S(2)}, u32[]{:S(2)}) collective-permute-start(bf16[32,2304]{1,0:T(8,128)(2,1)S(1)} %collective-permute-done.5.refs_10_), channel_id=1, source_target_pairs={{1,0},{2,1},{3,2},{4,3},{5,4},{6,5},{7,6},{0,7},{9,8},{10,9},{11,1... | collective-permute-start | bytes 442376 | tf_op jit(solution)/shard_map/ppermute | solution.py:283
  24.6 6.9 %collective-permute-start.8 = (bf16[32,2304]{1,0:T(8,128)(2,1)S(1)}, bf16[32,2304]{1,0:T(8,128)(2,1)S(1)}, u32[]{:S(2)}, u32[]{:S(2)}) collective-permute-start(bf16[32,2304]{1,0:T(8,128)(2,1)S(1)} %collective-permute-done.6.refs_4_), channel_id=1, source_target_pairs={{0,1},{1,2},{2,3},{3,4},{4,5},{5,6},{6,7},{7,0},{8,9},{9,10},{10,1... | collective-permute-start | bytes 442376 | tf_op jit(solution)/shard_map/ppermute | solution.py:283
  26.3 8.6 %collective-permute-start.13 = (bf16[32,2304]{1,0:T(8,128)(2,1)S(1)}, bf16[32,2304]{1,0:T(8,128)(2,1)S(1)}, u32[]{:S(2)}, u32[]{:S(2)}) collective-permute-start(bf16[32,2304]{1,0:T(8,128)(2,1)S(1)} %collective-permute-done.7.refs_5_), channel_id=1, source_target_pairs={{0,1},{1,2},{2,3},{3,4},{4,5},{5,6},{6,7},{7,0},{8,9},{9,10},{10,1... | collective-permute-start | bytes 442376 | tf_op jit(solution)/shard_map/ppermute | solution.py:304
  26.4 8.5 %collective-permute-start.14 = (bf16[32,2304]{1,0:T(8,128)(2,1)S(1)}, bf16[32,2304]{1,0:T(8,128)(2,1)S(1)}, u32[]{:S(2)}, u32[]{:S(2)}) collective-permute-start(bf16[32,2304]{1,0:T(8,128)(2,1)S(1)} %collective-permute-done.12.refs_13_), channel_id=1, source_target_pairs={{1,0},{2,1},{3,2},{4,3},{5,4},{6,5},{7,6},{0,7},{9,8},{10,9},{11,1... | collective-permute-start | bytes 442376 | tf_op jit(solution)/shard_map/ppermute | solution.py:305
  34.9 8.2 %collective-permute-start.16 = (f32[224,2304]{1,0:T(8,128)S(1)}, f32[224,2304]{1,0:T(8,128)S(1)}, u32[]{:S(2)}, u32[]{:S(2)}) collective-permute-start(f32[224,2304]{1,0:T(8,128)S(1)} %get-tuple-element.30), channel_id=1, source_target_pairs={{0,16},{16,0},{32,48},{48,32},{64,80},{80,64},{96,112},{112,96},{1... | collective-permute-start | bytes 6193160 | tf_op jit(solution)/shard_map/ppermute | solution.py:291
  41.6 2.0 %collective-permute-start.15 = (f32[32,2304]{1,0:T(8,128)S(1)}, f32[32,2304]{1,0:T(8,128)S(1)}, u32[]{:S(2)}, u32[]{:S(2)}) collective-permute-start(f32[32,2304]{1,0:T(8,128)S(1)} %get-tuple-element.28), channel_id=1, source_target_pairs={{0,16},{16,0},{32,48},{48,32},{64,80},{80,64},{96,112},{112,96},{1... | collective-permute-start | bytes 884744 | tf_op jit(solution)/shard_map/ppermute | solution.py:291
  69.5 22.9 %copy-start = (bf16[256,1792]{1,0:T(8,128)(2,1)S(1)}, bf16[256,1792]{1,0:T(8,128)(2,1)}, u32[]{:S(2)}) copy-start(bf16[256,1792]{1,0:T(8,128)(2,1)} %refs_1_.3) | copy-start | bytes 2752516
  69.6 22.9 %copy-start.1 = (bf16[256,512]{1,0:T(8,128)(2,1)S(1)}, bf16[256,512]{1,0:T(8,128)(2,1)}, u32[]{:S(2)}) copy-start(bf16[256,512]{1,0:T(8,128)(2,1)} %refs_2_.3) | copy-start | bytes 786436
  89.6 5.4 %collective-permute-start.17 = (s16[8,32,2432]{2,1,0:T(8,128)(2,1)S(1)}, s16[8,32,2432]{2,1,0:T(8,128)(2,1)S(1)}, u32[]{:S(2)}, u32[]{:S(2)}) collective-permute-start(s16[8,32,2432]{2,1,0:T(8,128)(2,1)S(1)} %all_to_all.21.refs_0_), channel_id=1, source_target_pairs={{0,16},{16,0},{32,48},{48,32},{64,80},{80,64},{96,112},{112,96},{1... | collective-permute-start | bytes 3735560 | tf_op jit(solution)/shard_map/ppermute | solution.py:313
  96.0 21.2 %copy-start.2 = (s32[16]{0:T(128)S(1)}, s32[16]{0:T(128)}, u32[]{:S(2)}) copy-start(s32[16]{0:T(128)} %lengths.1) | copy-start | bytes 196

commit v5 on v4

--- a/solution.py
+++ b/solution.py
@@ -293,12 +293,12 @@
     a1 = hop((mine, mine))
     b1 = hop((other, other))
     a2 = hop(a1)
-    a2, basis_in, basis_out = lax.optimization_barrier(
-        (a2, *stage(basis_in, basis_out))
+    b2 = hop(b1)
+    b2, basis_in, basis_out = lax.optimization_barrier(
+        (b2, *stage(basis_in, basis_out))
     )
     basis_in = pltpu.with_memory_space_constraint(basis_in, pltpu.VMEM)
     basis_out = pltpu.with_memory_space_constraint(basis_out, pltpu.VMEM)
-    b2 = hop(b1)
     a3 = hop(a2)
     b3 = hop(b2)
     a4 = lax.ppermute(a3[0], "inp", UP)

time: 132 us -> 136 us (1.030)
  blocking collectives: 79.9 us -> 82 us
  starting transfers between devices: 31.9 us -> 33.4 us
    all_to_all x1, blocking collectives: 21.2 us -> 22.9 us  [per_device(): sides = lax.all_to_all(sides, 'inp', 0, 0, tiled=True)]
    ppermute x2, starting transfers between devices: 4.59 us -> 6.23 us  [finish(): return code(keep, lax.ppermute(send, 'out', CORES), in_width, *done)]
  transfers between devices with their start and end apart: 18 -> 18, of which waited for: 7 -> 6; matrix products, arithmetic and copies ran while one was open for 0% -> 0% of each run, Pallas kernels for 8% -> 7%
where the time goes in v5:
time: 136 us
  blocking collectives  82 us (60%)
  starting transfers between devices  33.4 us (25%)
  Pallas kernels  12.7 us (9%)
  waiting for transfers between devices  6.4 us (5%)
  other arithmetic  1.48 us (1%)
    all_to_all x2, blocking collectives, per_device(): lax.all_to_all(codes, 'out', 0, 0, tiled=True, axis_index_groups=CHIPS)  45.2 us
    all_to_all x1, blocking collectives, per_device(): sides = lax.all_to_all(sides, 'inp', 0, 0, tiled=True)  22.9 us
    ppermute x12, starting transfers between devices, hop(): return (lax.ppermute(up, 'inp', UP), lax.ppermute(down, 'inp', DOWN))  19.5 us
    all_to_all x1, blocking collectives, per_device(): sums = lax.all_to_all(sums, 'out', 0, 0, tiled=True)  13.9 us
    ppermute x2, starting transfers between devices, finish(): return code(keep, lax.ppermute(send, 'out', CORES), in_width, *done)  6.23 us
    pallas_call x2, Pallas kernels, rotate(): pl.pallas_call(functools.partial(rotate_kernel, count), in_specs=[VMEM] *...  5.58 us
    pallas_call x1, Pallas kernels, stage(): pl.pallas_call(stage_kernel, in_specs=[pl.BlockSpec(memory_space=pltpu.HB...  2.98 us
    ppermute x1, starting transfers between devices, per_device(): sibling = lax.ppermute(own, 'out', CORES)  2.86 us
  transfers between devices with their start and end apart: 18, of which 6 were waited for; matrix products, arithmetic and copies ran while one was open for 0% of the time, Pallas kernels for 7%

profile of v5, /device:TPU:1, one launch (start us, length us, event | category | flops | bytes accessed | tf_op | source)
XLA Modules:
  0.0 136.2 jit_solution(10657479962465082766)
XLA Ops:
  0.9 2.1 %collective-permute-start.1 = (bf16[32,2304]{1,0:T(8,128)(2,1)S(1)}, bf16[32,2304]{1,0:T(8,128)(2,1)S(1)}, u32[]{:S(2)}, u32[]{:S(2)}) collective-permute-start(bf16[32,2304]{1,0:T(8,128)(2,1)S(1)} %pad_maximum_fusion.refs_0_), channel_id=1, source_target_pairs={{0,8},{1,9},{2,10},{3,11},{4,12},{5,13},{6,14},{7,15},{8,0},{9,1},... | collective-permute-start | bytes 442376 | tf_op jit(solution)/shard_map/ppermute | solution.py:278
  3.1 1.6 %collective-permute-start = (bf16[32,2304]{1,0:T(8,128)(2,1)S(1)}, bf16[32,2304]{1,0:T(8,128)(2,1)S(1)}, u32[]{:S(2)}, u32[]{:S(2)}) collective-permute-start(bf16[32,2304]{1,0:T(8,128)(2,1)S(1)} %pad_maximum_fusion.refs_0_), channel_id=1, source_target_pairs={{0,1},{1,2},{2,3},{3,4},{4,5},{5,6},{6,7},{7,0},{8,9},{9,10},{10,1... | collective-permute-start | bytes 442376 | tf_op jit(solution)/shard_map/ppermute | solution.py:283
  5.6 2.6 %collective-permute-start.2 = (bf16[32,2304]{1,0:T(8,128)(2,1)S(1)}, bf16[32,2304]{1,0:T(8,128)(2,1)S(1)}, u32[]{:S(2)}, u32[]{:S(2)}) collective-permute-start(bf16[32,2304]{1,0:T(8,128)(2,1)S(1)} %collective-permute-done.1.refs_7_), channel_id=1, source_target_pairs={{0,1},{1,2},{2,3},{3,4},{4,5},{5,6},{6,7},{7,0},{8,9},{9,10},{10,1... | collective-permute-start | bytes 442376 | tf_op jit(solution)/shard_map/ppermute | solution.py:283
  8.2 3.9 %collective-permute-start.5 = (bf16[32,2304]{1,0:T(8,128)(2,1)S(1)}, bf16[32,2304]{1,0:T(8,128)(2,1)S(1)}, u32[]{:S(2)}, u32[]{:S(2)}) collective-permute-start(bf16[32,2304]{1,0:T(8,128)(2,1)S(1)} %collective-permute-done.1.refs_7_), channel_id=1, source_target_pairs={{1,0},{2,1},{3,2},{4,3},{5,4},{6,5},{7,6},{0,7},{9,8},{10,9},{11,1... | collective-permute-start | bytes 442376 | tf_op jit(solution)/shard_map/ppermute | solution.py:283
  12.1 1.5 %collective-permute-start.9 = (bf16[32,2304]{1,0:T(8,128)(2,1)S(1)}, bf16[32,2304]{1,0:T(8,128)(2,1)S(1)}, u32[]{:S(2)}, u32[]{:S(2)}) collective-permute-start(bf16[32,2304]{1,0:T(8,128)(2,1)S(1)} %pad_maximum_fusion.refs_0_), channel_id=1, source_target_pairs={{1,0},{2,1},{3,2},{4,3},{5,4},{6,5},{7,6},{0,7},{9,8},{10,9},{11,1... | collective-permute-start | bytes 442376 | tf_op jit(solution)/shard_map/ppermute | solution.py:283
  13.6 1.0 collective-permute-done.2.refs_2_
  14.7 2.7 %collective-permute-start.6 = (bf16[32,2304]{1,0:T(8,128)(2,1)S(1)}, bf16[32,2304]{1,0:T(8,128)(2,1)S(1)}, u32[]{:S(2)}, u32[]{:S(2)}) collective-permute-start(bf16[32,2304]{1,0:T(8,128)(2,1)S(1)} %collective-permute-done.5.refs_9_), channel_id=1, source_target_pairs={{1,0},{2,1},{3,2},{4,3},{5,4},{6,5},{7,6},{0,7},{9,8},{10,9},{11,1... | collective-permute-start | bytes 442376 | tf_op jit(solution)/shard_map/ppermute | solution.py:283
  17.4 3.0 %collective-permute-start.10 = (bf16[32,2304]{1,0:T(8,128)(2,1)S(1)}, bf16[32,2304]{1,0:T(8,128)(2,1)S(1)}, u32[]{:S(2)}, u32[]{:S(2)}) collective-permute-start(bf16[32,2304]{1,0:T(8,128)(2,1)S(1)} %collective-permute-done.9.refs_8_), channel_id=1, source_target_pairs={{1,0},{2,1},{3,2},{4,3},{5,4},{6,5},{7,6},{0,7},{9,8},{10,9},{11,1... | collective-permute-start | bytes 442376 | tf_op jit(solution)/shard_map/ppermute | solution.py:283
  20.3 3.0 %shard_map.73 = (bf16[1792,1792]{1,0:T(8,128)(2,1)S(1)}, bf16[512,512]{1,0:T(8,128)(2,1)S(1)}) custom-call(bf16[1792,1792]{1,0:T(8,128)(2,1)} %basis_in.1, bf16[512,512]{1,0:T(8,128)(2,1)} %basis_out.1), custom_call_target="tpu_custom_call" | custom-call | flops 100000000 | bytes 100000 | tf_op jit(solution)/shard_map/pallas_call | solution.py:70
  23.4 2.6 %collective-permute-start.12 = (bf16[32,2304]{1,0:T(8,128)(2,1)S(1)}, bf16[32,2304]{1,0:T(8,128)(2,1)S(1)}, u32[]{:S(2)}, u32[]{:S(2)}) collective-permute-start(bf16[32,2304]{1,0:T(8,128)(2,1)S(1)} %collective-permute-done.6.refs_11_), channel_id=1, source_target_pairs={{1,0},{2,1},{3,2},{4,3},{5,4},{6,5},{7,6},{0,7},{9,8},{10,9},{11,1... | collective-permute-start | bytes 442376 | tf_op jit(solution)/shard_map/ppermute | solution.py:283
  26.2 1.4 %collective-permute-start.8 = (bf16[32,2304]{1,0:T(8,128)(2,1)S(1)}, bf16[32,2304]{1,0:T(8,128)(2,1)S(1)}, u32[]{:S(2)}, u32[]{:S(2)}) collective-permute-start(bf16[32,2304]{1,0:T(8,128)(2,1)S(1)} %collective-permute-done.4.refs_4_), channel_id=1, source_target_pairs={{0,1},{1,2},{2,3},{3,4},{4,5},{5,6},{6,7},{7,0},{8,9},{9,10},{10,1... | collective-permute-start | bytes 442376 | tf_op jit(solution)/shard_map/ppermute | solution.py:283
  27.5 1.0 collective-permute-done.7.refs_5_
  28.6 2.7 %collective-permute-start.14 = (bf16[32,2304]{1,0:T(8,128)(2,1)S(1)}, bf16[32,2304]{1,0:T(8,128)(2,1)S(1)}, u32[]{:S(2)}, u32[]{:S(2)}) collective-permute-start(bf16[32,2304]{1,0:T(8,128)(2,1)S(1)} %collective-permute-done.12.refs_13_), channel_id=1, source_target_pairs={{1,0},{2,1},{3,2},{4,3},{5,4},{6,5},{7,6},{0,7},{9,8},{10,9},{11,1... | collective-permute-start | bytes 442376 | tf_op jit(solution)/shard_map/ppermute | solution.py:305
  31.7 3.4 %shard_map.74 = (f32[224,2304]{1,0:T(8,128)S(1)}, f32[224,2304]{1,0:T(8,128)S(1)}) custom-call(bf16[32,2304]{1,0:T(8,128)(2,1)S(1)} %pad_maximum_fusion.refs_0_, bf16[32,2304]{1,0:T(8,128)(2,1)S(1)} %collective-permute-done.refs_1_, bf16[32,2304]{1,0:T(8,128)(2,1)S(1)} %collective-permute-done.2.refs_2_, ...), custom_call_target="tpu_custom_call" | custom-call | flops 3112173568 | bytes 100000 | tf_op jit(solution)/shard_map/pallas_call | solution.py:112
  35.1 6.1 %collective-permute-start.16 = (f32[224,2304]{1,0:T(8,128)S(1)}, f32[224,2304]{1,0:T(8,128)S(1)}, u32[]{:S(2)}, u32[]{:S(2)}) collective-permute-start(f32[224,2304]{1,0:T(8,128)S(1)} %get-tuple-element.30), channel_id=1, source_target_pairs={{0,16},{16,0},{32,48},{48,32},{64,80},{80,64},{96,112},{112,96},{1... | collective-permute-start | bytes 6193160 | tf_op jit(solution)/shard_map/ppermute | solution.py:291
  41.2 2.2 %shard_map.75 = (f32[32,2304]{1,0:T(8,128)S(1)}, f32[32,2304]{1,0:T(8,128)S(1)}) custom-call(bf16[32,2304]{1,0:T(8,128)(2,1)S(1)} %collective-permute-done.13.refs_0_, bf16[32,2304]{1,0:T(8,128)(2,1)S(1)} %collective-permute-done.14.refs_1_, bf16[1792,1792]{1,0:T(8,128)(2,1)S(1)} %get-tuple-element.22.refs_14_.refs_2_, ...), custom_call_target="tpu_custom_call" | custom-call | flops 444596224 | bytes 100000 | tf_op jit(solution)/shard_map/pallas_call | solution.py:112
  43.5 1.4 %collective-permute-done.16.got = f32[224,2304]{1,0:T(8,128)S(1)} collective-permute-done((f32[224,2304]{1,0:T(8,128)S(1)}, f32[224,2304]{1,0:T(8,128)S(1)}, u32[]{:S(2)}, u32[]{:S(2)}) %collective-permute-start.16) | collective-permute-done | bytes 2064416 | tf_op jit(solution)/shard_map/ppermute | solution.py:291
  45.7 25.2 %all_to_all.20.codes = s16[8,32,2432]{2,1,0:T(8,128)(2,1)S(1)} all-to-all(s16[8,32,2432]{2,1,0:T(8,128)(2,1)S(1)} %shard_map.77), channel_id=1, replica_groups={{0,32,64,96,128,160,192,224},{16,48,80,112,144,176,208,240},{1,33,65,97..., dimensions={0} | all-to-all | bytes 2490368 | tf_op jit(solution)/shard_map/all_to_all | solution.py:310
  71.4 20.0 %all_to_all.21.refs_0_ = s16[8,32,2432]{2,1,0:T(8,128)(2,1)S(1)} all-to-all(s16[8,32,2432]{2,1,0:T(8,128)(2,1)S(1)} %shard_map.78), channel_id=1, replica_groups={{0,32,64,96,128,160,192,224},{16,48,80,112,144,176,208,240},{1,33,65,97..., dimensions={0} | all-to-all | bytes 2490368 | tf_op jit(solution)/shard_map/all_to_all | solution.py:312
  91.4 2.9 %collective-permute-start.17 = (s16[8,32,2432]{2,1,0:T(8,128)(2,1)S(1)}, s16[8,32,2432]{2,1,0:T(8,128)(2,1)S(1)}, u32[]{:S(2)}, u32[]{:S(2)}) collective-permute-start(s16[8,32,2432]{2,1,0:T(8,128)(2,1)S(1)} %all_to_all.21.refs_0_), channel_id=1, source_target_pairs={{0,16},{16,0},{32,48},{48,32},{64,80},{80,64},{96,112},{112,96},{1... | collective-permute-start | bytes 3735560 | tf_op jit(solution)/shard_map/ppermute | solution.py:313
  95.3 1.6 %collective-permute-done.17.refs_0_ = s16[8,32,2432]{2,1,0:T(8,128)(2,1)S(1)} collective-permute-done((s16[8,32,2432]{2,1,0:T(8,128)(2,1)S(1)}, s16[8,32,2432]{2,1,0:T(8,128)(2,1)S(1)}, u32[]{:S(2)}, u32[]{:S(2)}) %collective-permute-start.17) | collective-permute-done | bytes 1245216 | tf_op jit(solution)/shard_map/ppermute | solution.py:313
  96.8 1.0 shard_map.80
  97.9 22.9 %all_to_all.22.codes = s16[16,32,640]{2,1,0:T(8,128)(2,1)S(1)} all-to-all(s16[16,32,640]{2,1,0:T(8,128)(2,1)S(1)} %shard_map.80), channel_id=1, replica_groups=mesh['out'=16,'inp'=16] {'inp'}, dimensions={0} | all-to-all | bytes 1310720 | tf_op jit(solution)/shard_map/all_to_all | solution.py:315
  121.7 13.9 %all_to_all.23 = f32[16,8,128]{2,1,0:T(8,128)S(1)} all-to-all(f32[16,8,128]{2,1,0:T(8,128)S(1)} %shard_map.81), channel_id=1, replica_groups=mesh['out'=16,'inp'=16] {'out'}, dimensions={0} | all-to-all | bytes 131072 | tf_op jit(solution)/shard_map/all_to_all | solution.py:317
  (34 shorter events, 6.2 us)
Async XLA Ops:
  0.9 4.7 %collective-permute-start.1 = (bf16[32,2304]{1,0:T(8,128)(2,1)S(1)}, bf16[32,2304]{1,0:T(8,128)(2,1)S(1)}, u32[]{:S(2)}, u32[]{:S(2)}) collective-permute-start(bf16[32,2304]{1,0:T(8,128)(2,1)S(1)} %pad_maximum_fusion.refs_0_), channel_id=1, source_target_pairs={{0,8},{1,9},{2,10},{3,11},{4,12},{5,13},{6,14},{7,15},{8,0},{9,1},... | collective-permute-start | bytes 442376 | tf_op jit(solution)/shard_map/ppermute | solution.py:278
  3.1 10.6 %collective-permute-start = (bf16[32,2304]{1,0:T(8,128)(2,1)S(1)}, bf16[32,2304]{1,0:T(8,128)(2,1)S(1)}, u32[]{:S(2)}, u32[]{:S(2)}) collective-permute-start(bf16[32,2304]{1,0:T(8,128)(2,1)S(1)} %pad_maximum_fusion.refs_0_), channel_id=1, source_target_pairs={{0,1},{1,2},{2,3},{3,4},{4,5},{5,6},{6,7},{7,0},{8,9},{9,10},{10,1... | collective-permute-start | bytes 442376 | tf_op jit(solution)/shard_map/ppermute | solution.py:283
  5.6 9.1 %collective-permute-start.2 = (bf16[32,2304]{1,0:T(8,128)(2,1)S(1)}, bf16[32,2304]{1,0:T(8,128)(2,1)S(1)}, u32[]{:S(2)}, u32[]{:S(2)}) collective-permute-start(bf16[32,2304]{1,0:T(8,128)(2,1)S(1)} %collective-permute-done.1.refs_7_), channel_id=1, source_target_pairs={{0,1},{1,2},{2,3},{3,4},{4,5},{5,6},{6,7},{7,0},{8,9},{9,10},{10,1... | collective-permute-start | bytes 442376 | tf_op jit(solution)/shard_map/ppermute | solution.py:283
  8.2 6.5 %collective-permute-start.5 = (bf16[32,2304]{1,0:T(8,128)(2,1)S(1)}, bf16[32,2304]{1,0:T(8,128)(2,1)S(1)}, u32[]{:S(2)}, u32[]{:S(2)}) collective-permute-start(bf16[32,2304]{1,0:T(8,128)(2,1)S(1)} %collective-permute-done.1.refs_7_), channel_id=1, source_target_pairs={{1,0},{2,1},{3,2},{4,3},{5,4},{6,5},{7,6},{0,7},{9,8},{10,9},{11,1... | collective-permute-start | bytes 442376 | tf_op jit(solution)/shard_map/ppermute | solution.py:283
  12.1 5.2 %collective-permute-start.9 = (bf16[32,2304]{1,0:T(8,128)(2,1)S(1)}, bf16[32,2304]{1,0:T(8,128)(2,1)S(1)}, u32[]{:S(2)}, u32[]{:S(2)}) collective-permute-start(bf16[32,2304]{1,0:T(8,128)(2,1)S(1)} %pad_maximum_fusion.refs_0_), channel_id=1, source_target_pairs={{1,0},{2,1},{3,2},{4,3},{5,4},{6,5},{7,6},{0,7},{9,8},{10,9},{11,1... | collective-permute-start | bytes 442376 | tf_op jit(solution)/shard_map/ppermute | solution.py:283
  13.6 9.7 %collective-permute-start.3 = (bf16[32,2304]{1,0:T(8,128)(2,1)S(1)}, bf16[32,2304]{1,0:T(8,128)(2,1)S(1)}, u32[]{:S(2)}, u32[]{:S(2)}) collective-permute-start(bf16[32,2304]{1,0:T(8,128)(2,1)S(1)} %collective-permute-done.refs_1_), channel_id=1, source_target_pairs={{0,1},{1,2},{2,3},{3,4},{4,5},{5,6},{6,7},{7,0},{8,9},{9,10},{10,1... | collective-permute-start | bytes 442376 | tf_op jit(solution)/shard_map/ppermute | solution.py:283
  14.7 8.7 %collective-permute-start.4 = (bf16[32,2304]{1,0:T(8,128)(2,1)S(1)}, bf16[32,2304]{1,0:T(8,128)(2,1)S(1)}, u32[]{:S(2)}, u32[]{:S(2)}) collective-permute-start(bf16[32,2304]{1,0:T(8,128)(2,1)S(1)} %collective-permute-done.2.refs_2_), channel_id=1, source_target_pairs={{0,1},{1,2},{2,3},{3,4},{4,5},{5,6},{6,7},{7,0},{8,9},{9,10},{10,1... | collective-permute-start | bytes 442376 | tf_op jit(solution)/shard_map/ppermute | solution.py:283
  14.7 8.7 %collective-permute-start.6 = (bf16[32,2304]{1,0:T(8,128)(2,1)S(1)}, bf16[32,2304]{1,0:T(8,128)(2,1)S(1)}, u32[]{:S(2)}, u32[]{:S(2)}) collective-permute-start(bf16[32,2304]{1,0:T(8,128)(2,1)S(1)} %collective-permute-done.5.refs_9_), channel_id=1, source_target_pairs={{1,0},{2,1},{3,2},{4,3},{5,4},{6,5},{7,6},{0,7},{9,8},{10,9},{11,1... | collective-permute-start | bytes 442376 | tf_op jit(solution)/shard_map/ppermute | solution.py:283
  17.4 8.7 %collective-permute-start.10 = (bf16[32,2304]{1,0:T(8,128)(2,1)S(1)}, bf16[32,2304]{1,0:T(8,128)(2,1)S(1)}, u32[]{:S(2)}, u32[]{:S(2)}) collective-permute-start(bf16[32,2304]{1,0:T(8,128)(2,1)S(1)} %collective-permute-done.9.refs_8_), channel_id=1, source_target_pairs={{1,0},{2,1},{3,2},{4,3},{5,4},{6,5},{7,6},{0,7},{9,8},{10,9},{11,1... | collective-permute-start | bytes 442376 | tf_op jit(solution)/shard_map/ppermute | solution.py:283
  23.3 5.3 %collective-permute-start.7 = (bf16[32,2304]{1,0:T(8,128)(2,1)S(1)}, bf16[32,2304]{1,0:T(8,128)(2,1)S(1)}, u32[]{:S(2)}, u32[]{:S(2)}) collective-permute-start(bf16[32,2304]{1,0:T(8,128)(2,1)S(1)} %collective-permute-done.3.refs_3_), channel_id=1, source_target_pairs={{0,1},{1,2},{2,3},{3,4},{4,5},{5,6},{6,7},{7,0},{8,9},{9,10},{10,1... | collective-permute-start | bytes 442376 | tf_op jit(solution)/shard_map/ppermute | solution.py:283
  23.4 5.2 %collective-permute-start.12 = (bf16[32,2304]{1,0:T(8,128)(2,1)S(1)}, bf16[32,2304]{1,0:T(8,128)(2,1)S(1)}, u32[]{:S(2)}, u32[]{:S(2)}) collective-permute-start(bf16[32,2304]{1,0:T(8,128)(2,1)S(1)} %collective-permute-done.6.refs_11_), channel_id=1, source_target_pairs={{1,0},{2,1},{3,2},{4,3},{5,4},{6,5},{7,6},{0,7},{9,8},{10,9},{11,1... | collective-permute-start | bytes 442376 | tf_op jit(solution)/shard_map/ppermute | solution.py:283
  26.1 5.2 %collective-permute-start.11 = (bf16[32,2304]{1,0:T(8,128)(2,1)S(1)}, bf16[32,2304]{1,0:T(8,128)(2,1)S(1)}, u32[]{:S(2)}, u32[]{:S(2)}) collective-permute-start(bf16[32,2304]{1,0:T(8,128)(2,1)S(1)} %collective-permute-done.10.refs_10_), channel_id=1, source_target_pairs={{1,0},{2,1},{3,2},{4,3},{5,4},{6,5},{7,6},{0,7},{9,8},{10,9},{11,1... | collective-permute-start | bytes 442376 | tf_op jit(solution)/shard_map/ppermute | solution.py:283
  26.2 5.5 %collective-permute-start.8 = (bf16[32,2304]{1,0:T(8,128)(2,1)S(1)}, bf16[32,2304]{1,0:T(8,128)(2,1)S(1)}, u32[]{:S(2)}, u32[]{:S(2)}) collective-permute-start(bf16[32,2304]{1,0:T(8,128)(2,1)S(1)} %collective-permute-done.4.refs_4_), channel_id=1, source_target_pairs={{0,1},{1,2},{2,3},{3,4},{4,5},{5,6},{6,7},{7,0},{8,9},{9,10},{10,1... | collective-permute-start | bytes 442376 | tf_op jit(solution)/shard_map/ppermute | solution.py:283
  28.6 6.5 %collective-permute-start.13 = (bf16[32,2304]{1,0:T(8,128)(2,1)S(1)}, bf16[32,2304]{1,0:T(8,128)(2,1)S(1)}, u32[]{:S(2)}, u32[]{:S(2)}) collective-permute-start(bf16[32,2304]{1,0:T(8,128)(2,1)S(1)} %collective-permute-done.7.refs_5_), channel_id=1, source_target_pairs={{0,1},{1,2},{2,3},{3,4},{4,5},{5,6},{6,7},{7,0},{8,9},{9,10},{10,1... | collective-permute-start | bytes 442376 | tf_op jit(solution)/shard_map/ppermute | solution.py:304
  28.6 6.5 %collective-permute-start.14 = (bf16[32,2304]{1,0:T(8,128)(2,1)S(1)}, bf16[32,2304]{1,0:T(8,128)(2,1)S(1)}, u32[]{:S(2)}, u32[]{:S(2)}) collective-permute-start(bf16[32,2304]{1,0:T(8,128)(2,1)S(1)} %collective-permute-done.12.refs_13_), channel_id=1, source_target_pairs={{1,0},{2,1},{3,2},{4,3},{5,4},{6,5},{7,6},{0,7},{9,8},{10,9},{11,1... | collective-permute-start | bytes 442376 | tf_op jit(solution)/shard_map/ppermute | solution.py:305
  35.1 9.9 %collective-permute-start.16 = (f32[224,2304]{1,0:T(8,128)S(1)}, f32[224,2304]{1,0:T(8,128)S(1)}, u32[]{:S(2)}, u32[]{:S(2)}) collective-permute-start(f32[224,2304]{1,0:T(8,128)S(1)} %get-tuple-element.30), channel_id=1, source_target_pairs={{0,16},{16,0},{32,48},{48,32},{64,80},{80,64},{96,112},{112,96},{1... | collective-permute-start | bytes 6193160 | tf_op jit(solution)/shard_map/ppermute | solution.py:291
  43.4 2.0 %collective-permute-start.15 = (f32[32,2304]{1,0:T(8,128)S(1)}, f32[32,2304]{1,0:T(8,128)S(1)}, u32[]{:S(2)}, u32[]{:S(2)}) collective-permute-start(f32[32,2304]{1,0:T(8,128)S(1)} %get-tuple-element.28), channel_id=1, source_target_pairs={{0,16},{16,0},{32,48},{48,32},{64,80},{80,64},{96,112},{112,96},{1... | collective-permute-start | bytes 884744 | tf_op jit(solution)/shard_map/ppermute | solution.py:291
  71.4 22.9 %copy-start = (bf16[256,1792]{1,0:T(8,128)(2,1)S(1)}, bf16[256,1792]{1,0:T(8,128)(2,1)}, u32[]{:S(2)}) copy-start(bf16[256,1792]{1,0:T(8,128)(2,1)} %refs_1_.3) | copy-start | bytes 2752516
  71.4 22.9 %copy-start.1 = (bf16[256,512]{1,0:T(8,128)(2,1)S(1)}, bf16[256,512]{1,0:T(8,128)(2,1)}, u32[]{:S(2)}) copy-start(bf16[256,512]{1,0:T(8,128)(2,1)} %refs_2_.3) | copy-start | bytes 786436
  91.4 5.4 %collective-permute-start.17 = (s16[8,32,2432]{2,1,0:T(8,128)(2,1)S(1)}, s16[8,32,2432]{2,1,0:T(8,128)(2,1)S(1)}, u32[]{:S(2)}, u32[]{:S(2)}) collective-permute-start(s16[8,32,2432]{2,1,0:T(8,128)(2,1)S(1)} %all_to_all.21.refs_0_), channel_id=1, source_target_pairs={{0,16},{16,0},{32,48},{48,32},{64,80},{80,64},{96,112},{112,96},{1... | collective-permute-start | bytes 3735560 | tf_op jit(solution)/shard_map/ppermute | solution.py:313
  97.8 23.0 %copy-start.2 = (s32[16]{0:T(128)S(1)}, s32[16]{0:T(128)}, u32[]{:S(2)}) copy-start(s32[16]{0:T(128)} %lengths.1) | copy-start | bytes 196
